TPU v7x, 32 devices: a whole 2x2x4 slice. The times are simulated.
32 devices in a mesh: dp: 16 (over z, y, x), mp: 2 (over core).
Axes of the slice: x: 2, y: 2, z: 4, core: 2. Of those that a mesh axis runs over, the one named last changes fastest.
Arguments:
- layer_input: bfloat16 [8192, 8192], P('dp', 'mp')
- norm_gain: bfloat16 [8192], P('mp'), may hold values from 0.5 to 1.5
- value_weight: bfloat16 [1024, 8192], P('dp', 'mp'), may hold values from -0.0625 to 0.0625
- value_cotangent: bfloat16 [8192, 1024], P('dp', 'mp')
- doc_ids: int32 [8192], P('dp'), may hold values from 0 to 31, never falling along the last dimension, each value on 1 to 512 neighbouring positions
- owners: int32 [16], replicated, may hold values from 0 to 15, as said below
- noise_seeds: int32 [16], replicated, may hold values from 0 to 1073741823
- master: float32 [4096, 8192], P('dp', 'mp'), may hold values from -0.12 to 0.12
- moment_one: float32 [4096, 8192], P('dp', 'mp'), may hold values from -6 to 6
- moment_two: float32 [4096, 8192], P('dp', 'mp'), may hold values from 0.5 to 8
Outputs:
- input_grad: bfloat16 [8192, 8192], P('dp', 'mp')
- new_master: float32 [4096, 8192], P('dp', 'mp')
- new_moment_one: float32 [4096, 8192], P('dp', 'mp')
- new_moment_two: float32 [4096, 8192], P('dp', 'mp')
Inputs may be any that keep to these rules, and one draw needn't show every extreme that they name: `owners`: each index of dp is named by at most 4 entries, and one is named by exactly 4.
All inputs are finite; a program needn't handle non-finite values.
Results may differ from a plain program's by a relative error of at most 0.0016.
Values may be sent and summed in bfloat16 or wider, within the bound.
A program may use at most 128 MiB of HBM per device.

v0:
```python
import jax
import jax.numpy as jnp
from jax import lax
from jax.sharding import PartitionSpec as P

EPS_NORM = 1e-06
CLIP_NORM = 128.0
NOISE_MULT = 0.01
LEARN_RATE = 0.001
BETA_ONE = 0.9
BETA_TWO = 0.999
ADAM_STEP = 100
ADAM_EPS = 1e-08


def mix_bits(bits_in):
    bits_in = jnp.bitwise_xor(bits_in, lax.shift_right_logical(bits_in, jnp.int32(16)))
    bits_in = bits_in * jnp.int32(2146121005)
    bits_in = jnp.bitwise_xor(bits_in, lax.shift_right_logical(bits_in, jnp.int32(15)))
    bits_in = bits_in * jnp.int32(-2073254261)
    bits_in = jnp.bitwise_xor(bits_in, lax.shift_right_logical(bits_in, jnp.int32(16)))
    return bits_in


def unit_draw(seed_value, position):
    hashed = mix_bits(mix_bits(jnp.bitwise_xor(position, seed_value)) + seed_value)
    return (lax.shift_right_logical(hashed, jnp.int32(8)).astype(jnp.float32) + 0.5) * (
        1.0 / 16777216.0
    )


def gauss_noise(seed_value, position):
    draw_one = unit_draw(seed_value, 2 * position)
    draw_two = unit_draw(seed_value, 2 * position + 1)
    return jnp.sqrt(-2.0 * jnp.log(draw_one)) * jnp.cos(6.283185307179586 * draw_two)


def body(
    layer_input,
    norm_gain,
    value_weight,
    value_cotangent,
    doc_ids,
    owners,
    noise_seeds,
    master,
    moment_one,
    moment_two,
):
    part_width = layer_input.shape[1]
    full_width = part_width * lax.axis_size("mp")
    group_rows = value_weight.shape[0]
    slot_count = master.shape[0] // group_rows
    cycle_size = lax.axis_size("dp")
    my_group = lax.axis_index("dp")
    my_column = lax.axis_index("mp")
    inputs = layer_input.astype(jnp.float32)
    gain_row = norm_gain.astype(jnp.float32)
    squares = lax.psum(jnp.sum(inputs * inputs, axis=1), "mp")
    inv_rms = lax.rsqrt(squares / full_width + EPS_NORM)[:, None]
    normed = (inputs * inv_rms * gain_row).astype(jnp.bfloat16)
    full_cot = lax.all_gather(value_cotangent, "mp", axis=1, tiled=True)
    cot_columns = full_cot
    dnormed = jnp.dot(
        cot_columns,
        lax.all_gather(value_weight, "dp", axis=0, tiled=True),
        preferred_element_type=jnp.float32,
    )
    weighted = gain_row * dnormed
    inner_part = jnp.sum(weighted * inputs, axis=1)
    same_doc = (doc_ids[:, None] == doc_ids[None, :]).astype(jnp.float32)
    gram_part = jnp.dot(normed, normed.T, preferred_element_type=jnp.float32)
    gram_values = jnp.dot(full_cot, full_cot.T, preferred_element_type=jnp.float32)
    gram_features, inner_sum = lax.psum((gram_part, inner_part), "mp")
    mine_sums = jnp.sum(same_doc * gram_features * gram_values, axis=1)
    input_grad = (
        inv_rms * weighted
        - inputs * inv_rms * inv_rms * inv_rms * (inner_sum / full_width)[:, None]
    ).astype(jnp.bfloat16)
    squared = jnp.dot(same_doc, mine_sums, precision=lax.Precision.HIGHEST)
    scales = CLIP_NORM / (jnp.sqrt(squared) + 0.01)
    clipped = (full_cot.astype(jnp.float32) * scales[:, None]).astype(jnp.bfloat16)
    row_pos = jnp.arange(group_rows, dtype=jnp.int32)[:, None]
    col_pos = my_column * part_width + jnp.arange(part_width, dtype=jnp.int32)[None, :]
    positions = row_pos * full_width + col_pos
    group_ids = jnp.arange(cycle_size, dtype=jnp.int32)
    earlier = group_ids[:, None] > group_ids[None, :]
    same_owner = owners[:, None] == owners[None, :]
    slot_rank = jnp.sum((earlier & same_owner).astype(jnp.int32), axis=1)
    slot_ids = jnp.arange(slot_count, dtype=jnp.int32)
    holds_slot = (owners[None, :] == my_group) & (slot_rank[None, :] == slot_ids[:, None])
    sources = jnp.sum(jnp.where(holds_slot, group_ids[None, :], 0), axis=1)
    filled = jnp.any(holds_slot, axis=1)
    filled_rows = jnp.repeat(filled, group_rows)
    cot_columns = clipped
    grad_tile = lax.psum_scatter(
        lax.dot_general(
            cot_columns, normed, (((0,), (0,)), ((), ())), preferred_element_type=jnp.float32
        ),
        "dp",
        scatter_dimension=0,
        tiled=True,
    )
    seed_value = noise_seeds[my_group]
    noisy_tile = grad_tile + NOISE_MULT * CLIP_NORM * gauss_noise(seed_value, positions)
    outgoing = jnp.where((group_ids == owners[my_group])[:, None, None], noisy_tile[None], 0.0)
    arrived = lax.all_to_all(outgoing, "dp", split_axis=0, concat_axis=0, tiled=True)
    gathered = jnp.take(arrived, sources, axis=0).reshape(slot_count * group_rows, part_width)
    first_new = BETA_ONE * moment_one + (1.0 - BETA_ONE) * gathered
    second_new = BETA_TWO * moment_two + (1.0 - BETA_TWO) * gathered * gathered
    update = (
        first_new
        / (1.0 - BETA_ONE**ADAM_STEP)
        / (jnp.sqrt(second_new / (1.0 - BETA_TWO**ADAM_STEP)) + ADAM_EPS)
    )
    master_new = master - LEARN_RATE * update
    keep_mask = filled_rows[:, None]
    new_master = jnp.where(keep_mask, master_new, master)
    new_moment_one = jnp.where(keep_mask, first_new, moment_one)
    new_moment_two = jnp.where(keep_mask, second_new, moment_two)
    return (input_grad, new_master, new_moment_one, new_moment_two)


def solution(mesh):
    in_specs = (
        P("dp", "mp"),
        P("mp"),
        P("dp", "mp"),
        P("dp", "mp"),
        P("dp"),
        P(),
        P(),
        P("dp", "mp"),
        P("dp", "mp"),
        P("dp", "mp"),
    )
    out_specs = (P("dp", "mp"), P("dp", "mp"), P("dp", "mp"), P("dp", "mp"))
    return jax.shard_map(body, mesh=mesh, in_specs=in_specs, out_specs=out_specs, check_vma=False)
```

profile of v0, /device:TPU:28, one launch (start us, length us, event | category | flops | bytes accessed | tf_op | source)
XLA Modules:
  0.0 970.8 jit_solution(16505997661258304326)
XLA Ops:
  7.2 0.7 all-gather.3.cloned.1.call-update
  7.9 0.7 all-gather.5.cloned.1.call-update
  8.7 0.7 convert_element_type.29
  9.4 10.4 %all-gather.3.cloned.1.call-done = bf16[512,1024]{1,0:T(8,128)(2,1)} async-done(((bf16[512,512]{1,0:T(8,128)(2,1)}), bf16[512,1024]{1,0:T(8,128)(2,1)}) %all-gather.3.cloned.1.call-update) | async-done | bytes 1048592 | tf_op jit(solution)/shard_map/all_gather | solution.py:62
  19.8 114.7 %all-gather.5.cloned.1.call-done = bf16[1024,4096]{1,0:T(8,128)(2,1)} async-done(((bf16[64,4096]{1,0:T(8,128)(2,1)}), bf16[1024,4096]{1,0:T(8,128)(2,1)}) %all-gather.5.cloned.1.call-update) | async-done | bytes 8388624 | tf_op jit(solution)/shard_map/all_gather | solution.py:66
  134.5 12.9 %fusion.7 = (f32[512]{0:T(512)S(1)}, f32[512]{0:T(512)S(1)}, f32[512,4096]{1,0:T(8,128)}) fusion(bf16[512,4096]{1,0:T(8,128)(2,1)} %param.10, f32[4096]{0:T(1024)S(1)} %convert_element_type.29, bf16[512,1024]{1,0:T(8,128)(2,1)} %all-gather.3.cloned.1.call-done, bf16[1024,4096]{1,0:T(8,128)(2,1)} %all-gather.5.cloned.1.call-done), kind=kOutput, calls=%fused_computation.11 | convolution fusion | flops 4307549184 | bytes 22040576 | tf_op jit(solution)/shard_map/dot_general | solution.py:64
  147.3 2.4 all-reduce
  149.8 7.0 fusion.17
  157.0 19.9 %all-reduce.3.cloned.1.call-done = f32[512,512]{1,0:T(8,128)} async-done(((f32[512,512]{1,0:T(8,128)}), f32[512,512]{1,0:T(8,128)}) %all-reduce.3.cloned.1.call-update) | async-done | bytes 1048592 | tf_op jit(solution)/shard_map/psum | solution.py:74
  176.9 2.2 fusion.14
  179.1 0.6 fusion.12
  179.8 8.4 fusion.15
  188.3 0.6 copy-done.3
  188.9 0.6 dynamic_slice.7
  189.5 0.6 dynamic_slice.6
  190.1 0.6 iota_compare_fusion.2
  190.7 348.7 %reduce-scatter.2.cloned.1.call-done = f32[64,4096]{1,0:T(8,128)} async-done(((f32[1024,4096]{1,0:T(8,128)}), f32[64,4096]{1,0:T(8,128)}) %reduce-scatter.2.cloned.1.call-update) | async-done | bytes 1048592 | tf_op jit(solution)/shard_map/reduce_scatter | solution.py:96
  539.4 7.3 multiply_add_fusion.1
  546.8 7.9 broadcast_select_fusion
  554.6 7.9 all-to-all-start
  563.3 7.4 fusion.5
  570.8 373.4 %all-to-all-done = f32[16,64,4096]{2,1,0:T(8,128)} async-done(((f32[16,64,4096]{2,1,0:T(8,128)}), f32[16,64,4096]{2,1,0:T(8,128)}, u32[]{:S(2)}, u32[]{:S(2)}) %all-to-all-start) | async-done | bytes 16777248 | tf_op jit(solution)/shard_map/all_to_all | solution.py:107
  944.1 8.5 gather_fusion
  952.6 11.6 %fusion.11 = (f32[256,4096]{1,0:T(8,128)}, f32[256,4096]{1,0:T(8,128)}, f32[256,4096]{1,0:T(8,128)}) fusion(f32[256,4096]{1,0:T(8,128)} %param.19, f32[4,64,4096]{2,1,0:T(8,128)} %gather_fusion, pred[256]{0:T(512)(128)(4,1)S(1)} %broadcast_in_dim.90, pred[256]{0:T(512)(128)(4,1)S(1)} %broadcast_in_dim.85, f32[256,4096]{1,0:T(8,128)} %param.17, ...), kind=kLoop, calls=%fused_computation.20 | loop fusion | flops 17825792 | bytes 29360640 | tf_op jit(solution)/shard_map/jit(_where)/select_n | solution.py:120
  (31 shorter events, 1.2 us)
Async XLA Ops:
  7.2 12.6 %all-gather.3.cloned.1.call-start = ((), (), s32[]{:S(2)}) async-start(), calls=%async_computation.2 | async-start | bytes 1572864 | tf_op jit(solution)/shard_map/all_gather | solution.py:62
  7.9 126.6 %all-gather.5.cloned.1.call-start = ((), (), s32[]{:S(2)}) async-start(), calls=%async_computation.3 | async-start | bytes 8912896 | tf_op jit(solution)/shard_map/all_gather | solution.py:66
  8.6 168.3 %all-reduce.3.cloned.1.call-start = ((), (), s32[]{:S(2)}) async-start(), calls=%async_computation.4 | async-start | bytes 2097152 | tf_op jit(solution)/shard_map/psum | solution.py:74
  149.8 27.1 %copy-start.1 = (bf16[512,1024]{1,0:T(8,128)(2,1)S(1)}, bf16[512,1024]{1,0:T(8,128)(2,1)}, u32[]{:S(2)}) copy-start(bf16[512,1024]{1,0:T(8,128)(2,1)} %all-gather.3.cloned.1.call-done) | copy-start | bytes 3145732
  149.8 27.1 %copy-start.2 = (s32[512]{0:T(512)S(1)}, s32[512]{0:T(512)}, u32[]{:S(2)}) copy-start(s32[512]{0:T(512)} %param.14) | copy-start | bytes 6148
  156.8 382.6 %reduce-scatter.2.cloned.1.call-start = ((), (), s32[]{:S(2)}) async-start(), calls=%async_computation.5 | async-start | bytes 17825792 | tf_op jit(solution)/shard_map/reduce_scatter | solution.py:96
  176.9 2.9 copy-start
  188.2 0.7 copy-start.3
  188.2 1.2 copy-start.4
  554.6 389.5 %all-to-all-start = ((f32[16,64,4096]{2,1,0:T(8,128)}), f32[16,64,4096]{2,1,0:T(8,128)}, u32[]{:S(2)}, u32[]{:S(2)}) async-start(f32[16,64,4096]{2,1,0:T(8,128)} %broadcast_select_fusion), calls=%async_computation.1 | async-start | bytes 33554432 | tf_op jit(solution)/shard_map/all_to_all | solution.py:107
Sparse Core Ops, SparseCore 0:
  9.5 10.2 all-gather.2
  22.6 111.8 all-gather.4
  156.9 19.9 all-reduce.2
  188.4 351.0 reduce-scatter.1
where the time goes:
time: 971 us
  waiting for transfers between devices  868 us (89%)
  other arithmetic  36 us (4%)
  matrix products  31.1 us (3%)
  between operations  13.8 us (1%)
  local copies, waits for them, and re-layouts  10.6 us (1%)
    all_to_all x1, waiting for transfers between devices, body(): lax.all_to_all(outgoing, 'dp', split_axis=0, concat_axis=0, tiled=True)  373 us
    reduce_scatter x1, waiting for transfers between devices, body(): lax.psum_scatter(lax.dot_general(cot_columns, normed, (((0,), (0,)), ((),...  349 us
    all_gather x1, waiting for transfers between devices, body(): lax.all_gather(value_weight, 'dp', axis=0, tiled=True)  115 us
    psum x1, waiting for transfers between devices, body(): gram_features, inner_sum = lax.psum((gram_part, inner_part), 'mp')  19.9 us
  transfers between devices with their start and end apart: 5, of which 5 were waited for; matrix products, arithmetic and copies ran while one was open for 1% of the time, Pallas kernels for 0%

commit v1 on v0

--- a/solution.py
+++ b/solution.py
@@ -1,6 +1,10 @@
+import functools
+
 import jax
 import jax.numpy as jnp
 from jax import lax
+from jax.experimental import pallas as pl
+from jax.experimental.pallas import tpu as pltpu
 from jax.sharding import PartitionSpec as P
 
 EPS_NORM = 1e-06
@@ -33,6 +37,381 @@
     draw_one = unit_draw(seed_value, 2 * position)
     draw_two = unit_draw(seed_value, 2 * position + 1)
     return jnp.sqrt(-2.0 * jnp.log(draw_one)) * jnp.cos(6.283185307179586 * draw_two)
+
+
+PLANE = 4
+
+
+class Links:
+    def __init__(self, planes):
+        self.planes = planes
+        me = lax.axis_index("dp")
+        self.mp = lax.axis_index("mp")
+        self.line = me // PLANE
+        self.row = (me // 2) % 2
+        self.col = me % 2
+
+    def index(self, line, row, col):
+        return line * PLANE + row * 2 + col
+
+    def col_peer(self):
+        return (self.index(self.line, self.row, 1 - self.col), self.mp)
+
+    def row_peer(self):
+        return (self.index(self.line, 1 - self.row, self.col), self.mp)
+
+    def above(self):
+        return (self.index(self.line + 1, self.row, self.col), self.mp)
+
+    def below(self):
+        return (self.index(self.line - 1, self.row, self.col), self.mp)
+
+    def has_above(self):
+        return self.line + 1 < self.planes
+
+    def has_below(self):
+        return self.line > 0
+
+    def greet(self):
+        barrier = pltpu.get_barrier_semaphore()
+        mesh_ids = pl.DeviceIdType.MESH
+        for peer in (self.col_peer(), self.row_peer()):
+            pl.semaphore_signal(barrier, inc=1, device_id=peer, device_id_type=mesh_ids)
+
+        @pl.when(self.has_above())
+        def _():
+            pl.semaphore_signal(barrier, inc=1, device_id=self.above(), device_id_type=mesh_ids)
+
+        @pl.when(self.has_below())
+        def _():
+            pl.semaphore_signal(barrier, inc=1, device_id=self.below(), device_id_type=mesh_ids)
+
+        ends = jnp.where(self.line > 0, 1, 0) + jnp.where(self.line + 1 < self.planes, 1, 0)
+        pl.semaphore_wait(barrier, 2 + ends)
+
+
+def remote(src, dst, send_sem, recv_sem, peer):
+    return pltpu.make_async_remote_copy(
+        src_ref=src,
+        dst_ref=dst,
+        send_sem=send_sem,
+        recv_sem=recv_sem,
+        device_id=peer,
+        device_id_type=pl.DeviceIdType.MESH,
+    )
+
+
+def gather_kernel(planes, tile_ref, out_ref, own_sem, send_sems, recv_sems):
+    links = Links(planes)
+    half = tile_ref.shape[1] // 2
+    mine = links.index(links.line, links.row, links.col)
+    own = pltpu.make_async_copy(tile_ref, out_ref.at[mine], own_sem)
+    own.start()
+    links.greet()
+    ways = (links.col_peer(), links.row_peer(), links.above(), links.below())
+    pending = []
+
+    def piece(shard, part):
+        return out_ref.at[shard, :, pl.ds(part * half, half)]
+
+    def transfer(shard, part, way, from_tile=False):
+        source = tile_ref.at[:, pl.ds(part * half, half)] if from_tile else piece(shard, part)
+        return remote(
+            source,
+            piece(shard, part),
+            send_sems.at[shard, part, way],
+            recv_sems.at[shard, part],
+            ways[way],
+        )
+
+    def start(shard, part, way, guard, from_tile=False):
+        copy = transfer(shard, part, way, from_tile)
+        pending.append((guard, copy))
+        if guard is None:
+            copy.start()
+        else:
+            pl.when(guard)(copy.start)
+
+    def arrive(shard, part, guard):
+        copy = transfer(shard, part, 0)
+        if guard is None:
+            copy.wait_recv()
+        else:
+            pl.when(guard)(copy.wait_recv)
+
+    def both(first, second):
+        return second if first is None else jnp.logical_and(first, second)
+
+    def spread(line, guard, from_tile):
+        shard = links.index(line, links.row, links.col)
+        start(shard, 0, 0, guard, from_tile)
+        start(shard, 1, 1, guard, from_tile)
+        start(shard, 0, 1, guard, from_tile)
+        start(shard, 1, 0, guard, from_tile)
+
+    def relay(line, guard):
+        shard = links.index(line, links.row, 1 - links.col)
+        arrive(shard, 0, guard)
+        start(shard, 0, 1, guard)
+        shard = links.index(line, 1 - links.row, links.col)
+        arrive(shard, 1, guard)
+        start(shard, 1, 0, guard)
+
+    for part in (0, 1):
+        start(mine, part, 2, links.has_above(), True)
+        start(mine, part, 3, links.has_below(), True)
+    spread(links.line, None, True)
+    lines = [[(links.line, None)]]
+    for step in range(1, planes):
+        from_below = links.line - step
+        from_above = links.line + step
+        got_below = from_below >= 0
+        got_above = from_above < planes
+        for part in (0, 1):
+            shard = links.index(from_below, links.row, links.col)
+            arrive(shard, part, got_below)
+            start(shard, part, 2, both(got_below, links.has_above()))
+            shard = links.index(from_above, links.row, links.col)
+            arrive(shard, part, got_above)
+            start(shard, part, 3, both(got_above, links.has_below()))
+        spread(from_below, got_below, False)
+        spread(from_above, got_above, False)
+        for line, guard in lines[-1]:
+            relay(line, guard)
+        lines.append([(from_below, got_below), (from_above, got_above)])
+    for line, guard in lines[-1]:
+        relay(line, guard)
+    for group in lines:
+        for line, guard in group:
+            for part in (0, 1):
+                arrive(links.index(line, 1 - links.row, 1 - links.col), part, guard)
+            arrive(links.index(line, 1 - links.row, links.col), 0, guard)
+            arrive(links.index(line, links.row, 1 - links.col), 1, guard)
+    for guard, copy in pending:
+        if guard is None:
+            copy.wait_send()
+        else:
+            pl.when(guard)(copy.wait_send)
+    own.wait()
+
+
+def gather_tiles(tile, count):
+    rows, width = tile.shape
+    return pl.pallas_call(
+        functools.partial(gather_kernel, count // PLANE),
+        out_shape=jax.ShapeDtypeStruct((count, rows, width), tile.dtype),
+        in_specs=[pl.BlockSpec(memory_space=pl.ANY)],
+        out_specs=pl.BlockSpec(memory_space=pl.ANY),
+        scratch_shapes=[
+            pltpu.SemaphoreType.DMA,
+            pltpu.SemaphoreType.DMA((count, 2, 4)),
+            pltpu.SemaphoreType.DMA((count, 2)),
+        ],
+        compiler_params=pltpu.CompilerParams(collective_id=1, has_side_effects=True),
+        cost_estimate=pl.CostEstimate(
+            flops=0, bytes_accessed=2 * count * rows * width * 2, transcendentals=0
+        ),
+    )(tile)
+
+
+def scatter_kernel(
+    planes,
+    part_ref,
+    out_ref,
+    first_in,
+    second_in,
+    line_in,
+    second_out,
+    line_out,
+    send_sems,
+    first_sems,
+    second_sems,
+    line_sems,
+):
+    links = Links(planes)
+    rows, width = out_ref.shape
+    half = width // 2
+    block = 16
+    links.greet()
+    pending = []
+    row, col, place = links.row, links.col, links.line
+    order = sorted(range(planes), key=lambda line: -max(line, planes - 1 - line))
+    first_peer = (links.row_peer(), links.col_peer())
+    second_peer = (links.col_peer(), links.row_peer())
+
+    def columns(part):
+        return pl.ds(part * half, half)
+
+    def first_copy(line, part):
+        if part == 0:
+            source = part_ref.at[line, 1 - row, :, :, columns(0)]
+        else:
+            source = part_ref.at[line, :, 1 - col, :, columns(1)]
+        return remote(
+            source,
+            first_in.at[line, part],
+            send_sems.at[line, part, 0],
+            first_sems.at[line, part],
+            first_peer[part],
+        )
+
+    def second_copy(line, part):
+        return remote(
+            second_out.at[line, part],
+            second_in.at[line, part],
+            send_sems.at[line, part, 1],
+            second_sems.at[line, part],
+            second_peer[part],
+        )
+
+    def line_copy(line, part, side):
+        return remote(
+            line_out.at[line, part],
+            line_in.at[side, line, part],
+            send_sems.at[line, part, 2],
+            line_sems.at[side, line, part],
+            links.above() if side == 0 else links.below(),
+        )
+
+    def send_first(line):
+        for part in (0, 1):
+            copy = first_copy(line, part)
+            copy.start()
+            pending.append((None, copy))
+
+    def by_blocks(step):
+        def at(index, carry):
+            step(pl.ds(pl.multiple_of(index * block, block), block))
+            return carry
+
+        lax.fori_loop(0, rows // block, at, 0)
+
+    def send_second(line):
+        for part in (0, 1):
+            first_copy(line, part).wait_recv()
+            give_row, give_col = (row, 1 - col) if part == 0 else (1 - row, col)
+            lane = 1 - col if part == 0 else 1 - row
+
+            def step(at):
+                second_out[line, part, at, :] = (
+                    part_ref[line, give_row, give_col, at, columns(part)].astype(jnp.float32)
+                    + first_in[line, part, lane, at, :].astype(jnp.float32)
+                ).astype(jnp.bfloat16)
+
+            by_blocks(step)
+            copy = second_copy(line, part)
+            copy.start()
+            pending.append((None, copy))
+
+    def plane_sum(line, part, at):
+        lane = col if part == 0 else row
+        return (
+            part_ref[line, row, col, at, columns(part)].astype(jnp.float32)
+            + first_in[line, part, lane, at, :].astype(jnp.float32)
+            + second_in[line, part, at, :].astype(jnp.float32)
+        )
+
+    def send_line(line):
+        for part in (0, 1):
+            second_copy(line, part).wait_recv()
+
+            @pl.when(place == line)
+            def _():
+                def step(at):
+                    out_ref[at, columns(part)] = plane_sum(line, part, at)
+
+                by_blocks(step)
+
+            for side, sends, joins in (
+                (0, place < line, place > 0),
+                (1, place > line, place < planes - 1),
+            ):
+
+                @pl.when(jnp.logical_and(sends, joins))
+                def _():
+                    line_copy(line, part, side).wait_recv()
+
+                    def step(at):
+                        line_out[line, part, at, :] = (
+                            plane_sum(line, part, at)
+                            + line_in[side, line, part, at, :].astype(jnp.float32)
+                        ).astype(jnp.bfloat16)
+
+                    by_blocks(step)
+
+                @pl.when(jnp.logical_and(sends, jnp.logical_not(joins)))
+                def _():
+                    def step(at):
+                        line_out[line, part, at, :] = plane_sum(line, part, at).astype(jnp.bfloat16)
+
+                    by_blocks(step)
+
+                copy = line_copy(line, part, side)
+                pl.when(sends)(copy.start)
+                pending.append((sends, copy))
+
+    ahead = 2
+    for line in order[:ahead]:
+        send_first(line)
+    for index, line in enumerate(order):
+        send_second(line)
+        if index + ahead < planes:
+            send_first(order[index + ahead])
+        if index > 0:
+            send_line(order[index - 1])
+    send_line(order[-1])
+
+    for side, joins in ((0, place > 0), (1, place < planes - 1)):
+        for part in (0, 1):
+
+            @pl.when(joins)
+            def _():
+                line_copy(place, part, side).wait_recv()
+
+                def step(at):
+                    out_ref[at, columns(part)] += line_in[side, place, part, at, :].astype(
+                        jnp.float32
+                    )
+
+                by_blocks(step)
+
+    for guard, copy in pending:
+        if guard is None:
+            copy.wait_send()
+        else:
+            pl.when(guard)(copy.wait_send)
+
+
+def scatter_sum(partial_tiles, count):
+    planes = count // PLANE
+    rows = partial_tiles.shape[0] // count
+    width = partial_tiles.shape[1]
+    half = width // 2
+    return pl.pallas_call(
+        functools.partial(scatter_kernel, planes),
+        out_shape=jax.ShapeDtypeStruct((rows, width), jnp.float32),
+        in_specs=[pl.BlockSpec(memory_space=pltpu.VMEM)],
+        out_specs=pl.BlockSpec(memory_space=pltpu.VMEM),
+        scratch_shapes=[
+            pltpu.VMEM((planes, 2, 2, rows, half), jnp.bfloat16),
+            pltpu.VMEM((planes, 2, rows, half), jnp.bfloat16),
+            pltpu.VMEM((2, planes, 2, rows, half), jnp.bfloat16),
+            pltpu.VMEM((planes, 2, rows, half), jnp.bfloat16),
+            pltpu.VMEM((planes, 2, rows, half), jnp.bfloat16),
+            pltpu.SemaphoreType.DMA((planes, 2, 3)),
+            pltpu.SemaphoreType.DMA((planes, 2)),
+            pltpu.SemaphoreType.DMA((planes, 2)),
+            pltpu.SemaphoreType.DMA((2, planes, 2)),
+        ],
+        compiler_params=pltpu.CompilerParams(
+            collective_id=2, has_side_effects=True, vmem_limit_bytes=40 * 1024 * 1024
+        ),
+        cost_estimate=pl.CostEstimate(
+            flops=4 * count * rows * width,
+            bytes_accessed=8 * count * rows * width,
+            transcendentals=0,
+        ),
+    )(partial_tiles.reshape(planes, 2, 2, rows, width))
 
 
 def body(
@@ -59,30 +438,21 @@
     squares = lax.psum(jnp.sum(inputs * inputs, axis=1), "mp")
     inv_rms = lax.rsqrt(squares / full_width + EPS_NORM)[:, None]
     normed = (inputs * inv_rms * gain_row).astype(jnp.bfloat16)
+    seed_value = noise_seeds[my_group]
+    row_pos = jnp.arange(group_rows, dtype=jnp.int32)[:, None]
+    col_pos = my_column * part_width + jnp.arange(part_width, dtype=jnp.int32)[None, :]
+    positions = row_pos * full_width + col_pos
+    noise = lax.optimization_barrier(NOISE_MULT * CLIP_NORM * gauss_noise(seed_value, positions))
+    full_weight = lax.all_gather(value_weight, "dp", axis=0, tiled=True)
     full_cot = lax.all_gather(value_cotangent, "mp", axis=1, tiled=True)
-    cot_columns = full_cot
-    dnormed = jnp.dot(
-        cot_columns,
-        lax.all_gather(value_weight, "dp", axis=0, tiled=True),
-        preferred_element_type=jnp.float32,
-    )
-    weighted = gain_row * dnormed
-    inner_part = jnp.sum(weighted * inputs, axis=1)
     same_doc = (doc_ids[:, None] == doc_ids[None, :]).astype(jnp.float32)
     gram_part = jnp.dot(normed, normed.T, preferred_element_type=jnp.float32)
     gram_values = jnp.dot(full_cot, full_cot.T, preferred_element_type=jnp.float32)
-    gram_features, inner_sum = lax.psum((gram_part, inner_part), "mp")
+    gram_features = lax.psum(gram_part, "mp")
     mine_sums = jnp.sum(same_doc * gram_features * gram_values, axis=1)
-    input_grad = (
-        inv_rms * weighted
-        - inputs * inv_rms * inv_rms * inv_rms * (inner_sum / full_width)[:, None]
-    ).astype(jnp.bfloat16)
     squared = jnp.dot(same_doc, mine_sums, precision=lax.Precision.HIGHEST)
     scales = CLIP_NORM / (jnp.sqrt(squared) + 0.01)
     clipped = (full_cot.astype(jnp.float32) * scales[:, None]).astype(jnp.bfloat16)
-    row_pos = jnp.arange(group_rows, dtype=jnp.int32)[:, None]
-    col_pos = my_column * part_width + jnp.arange(part_width, dtype=jnp.int32)[None, :]
-    positions = row_pos * full_width + col_pos
     group_ids = jnp.arange(cycle_size, dtype=jnp.int32)
     earlier = group_ids[:, None] > group_ids[None, :]
     same_owner = owners[:, None] == owners[None, :]
@@ -92,20 +462,22 @@
     sources = jnp.sum(jnp.where(holds_slot, group_ids[None, :], 0), axis=1)
     filled = jnp.any(holds_slot, axis=1)
     filled_rows = jnp.repeat(filled, group_rows)
-    cot_columns = clipped
-    grad_tile = lax.psum_scatter(
-        lax.dot_general(
-            cot_columns, normed, (((0,), (0,)), ((), ())), preferred_element_type=jnp.float32
-        ),
-        "dp",
-        scatter_dimension=0,
-        tiled=True,
-    )
-    seed_value = noise_seeds[my_group]
-    noisy_tile = grad_tile + NOISE_MULT * CLIP_NORM * gauss_noise(seed_value, positions)
-    outgoing = jnp.where((group_ids == owners[my_group])[:, None, None], noisy_tile[None], 0.0)
-    arrived = lax.all_to_all(outgoing, "dp", split_axis=0, concat_axis=0, tiled=True)
+    partial_grad = lax.dot_general(
+        clipped, normed, (((0,), (0,)), ((), ())), preferred_element_type=jnp.float32
+    ).astype(jnp.bfloat16)
+    grad_tile = scatter_sum(partial_grad, cycle_size)
+    noisy_tile = (grad_tile + noise).astype(jnp.bfloat16)
+    arrived = gather_tiles(noisy_tile, cycle_size)
+    late_cot, arrived = lax.optimization_barrier((full_cot, arrived))
+    dnormed = jnp.dot(late_cot, full_weight, preferred_element_type=jnp.float32)
+    weighted = gain_row * dnormed
+    inner_sum = lax.psum(jnp.sum(weighted * inputs, axis=1), "mp")
+    input_grad = (
+        inv_rms * weighted
+        - inputs * inv_rms * inv_rms * inv_rms * (inner_sum / full_width)[:, None]
+    ).astype(jnp.bfloat16)
     gathered = jnp.take(arrived, sources, axis=0).reshape(slot_count * group_rows, part_width)
+    gathered = gathered.astype(jnp.float32)
     first_new = BETA_ONE * moment_one + (1.0 - BETA_ONE) * gathered
     second_new = BETA_TWO * moment_two + (1.0 - BETA_TWO) * gathered * gathered
     update = (

time: 971 us -> 331 us (0.34)
  waiting for transfers between devices: 868 us -> 25.1 us
  Pallas kernels: 0 us -> 221 us
    all_to_all x1 -> x0, waiting for transfers between devices: 373 us -> none  [body(): lax.all_to_all(outgoing, 'dp', split_axis=0, concat_axis=0, tiled=True)]
    reduce_scatter x1 -> x0, waiting for transfers between devices: 349 us -> none  [body(): lax.psum_scatter(lax.dot_general(cot_columns, normed, (((0,), (0,)), ((),...]
    pallas_call x0 -> x2, Pallas kernels: none -> 221 us  [the longest x1 135 us: scatter_sum(): pl.pallas_call(functools.partial(scatter_kernel, planes), out_shape=jax.S...]
    all_gather x1, waiting for transfers between devices: 115 us -> 0.01 us  [body(): full_weight = lax.all_gather(value_weight, 'dp', axis=0, tiled=True)]
  transfers between devices with their start and end apart: 5 -> 3, of which waited for: 5 -> 2; matrix products, arithmetic and copies ran while one was open for 1% -> 10% of each run, Pallas kernels for 0% -> 67%
where the time goes in v1:
time: 331 us; the launch traced here: 327 us
  Pallas kernels  221 us (67%)
  other arithmetic  29.7 us (9%)
  matrix products  27.9 us (8%)
  waiting for transfers between devices  25.1 us (8%)
  between operations  13.9 us (4%)
  local copies, waits for them, and re-layouts  5 us (2%)
  blocking collectives  4.91 us (1%)
    pallas_call x1, Pallas kernels, scatter_sum(): pl.pallas_call(functools.partial(scatter_kernel, planes), out_shape=jax.S...  135 us
    pallas_call x1, Pallas kernels, gather_tiles(): pl.pallas_call(functools.partial(gather_kernel, count // PLANE), out_shap...  85.3 us
    psum x1, waiting for transfers between devices, body(): gram_features = lax.psum(gram_part, 'mp')  12.1 us
    all_gather x1, waiting for transfers between devices, body(): full_cot = lax.all_gather(value_cotangent, 'mp', axis=1, tiled=True)  11.9 us
    select_n x1, other arithmetic, body(): new_moment_two = jnp.where(keep_mask, second_new, moment_two)  11.1 us
    dot_general x1, matrix products, body(): dnormed = jnp.dot(late_cot, full_weight, preferred_element_type=jnp.float32)  11 us
    convert_element_type x1, other arithmetic, body(): input_grad = (inv_rms * weighted - inputs * inv_rms * inv_rms * inv_rms *...  7.43 us
    dot_general x1, matrix products, body(): gram_part = jnp.dot(normed, normed.T, preferred_element_type=jnp.float32)  6.92 us
  transfers between devices with their start and end apart: 3, of which 2 were waited for; matrix products, arithmetic and copies ran while one was open for 10% of the time, Pallas kernels for 67%

profile of v1, /device:TPU:28, one launch (start us, length us, event | category | flops | bytes accessed | tf_op | source)
XLA Modules:
  0.0 327.3 jit_solution(14329640200940711843)
XLA Ops:
  7.2 0.7 convert_element_type.38
  7.9 3.1 fusion.7
  11.0 2.5 psum.21
  13.5 6.9 %fusion.17 = f32[512,512]{1,0:T(8,128)} fusion(bf16[512,4096]{1,0:T(8,128)(2,1)} %param.10, f32[4096]{0:T(1024)S(1)} %convert_element_type.38, f32[512]{0:T(512)S(1)} %add_rsqrt_fusion), kind=kOutput, calls=%fused_computation.40 | convolution fusion | flops 2155872256 | bytes 5261312 | tf_op jit(solution)/shard_map/dot_general | solution.py:449
  20.5 0.7 all-gather.3.cloned.1.call-update
  21.2 0.2 all-gather.5.cloned.1.call-start
  21.4 0.5 all-gather.5.cloned.1.call-update
  21.9 0.6 dynamic_slice.3
  22.5 6.0 %fusion.42 = f32[64,4096]{1,0:T(8,128)S(1)} fusion(s32[]{:T(128)} %bitcast.3, s32[4096]{0:T(1024)S(1)} %iota_add_fusion, s32[64]{0:T(128)S(1)} %iota_multiply_fusion), kind=kLoop, calls=%fused_computation.65 | loop fusion | flops 13107200 | bytes 1065220 | tf_op jit(solution)/shard_map/mul | solution.py:445
  28.5 0.2 convert_reduce_fusion
  28.7 0.1 select_reduce_fusion
  29.3 12.1 %all-reduce.2.cloned.1.call-done = f32[512,512]{1,0:T(8,128)} async-done(((f32[512,512]{1,0:T(8,128)}), f32[512,512]{1,0:T(8,128)}) %all-reduce.2.cloned.1.call-update) | async-done | bytes 1048592 | tf_op jit(solution)/shard_map/psum | solution.py:451
  41.4 11.9 %all-gather.3.cloned.1.call-done = bf16[512,1024]{1,0:T(8,128)(2,1)} async-done(((bf16[512,512]{1,0:T(8,128)(2,1)}), bf16[512,1024]{1,0:T(8,128)(2,1)}) %all-gather.3.cloned.1.call-update) | async-done | bytes 1048592 | tf_op jit(solution)/shard_map/all_gather | solution.py:447
  53.2 2.8 fusion.15
  56.1 0.6 fusion.13
  56.7 6.5 %convolution_convert_fusion = bf16[1024,4096]{1,0:T(8,128)(2,1)S(1)} fusion(bf16[512,4096]{1,0:T(8,128)(2,1)S(1)} %copy-done, f32[4096]{0:T(1024)S(1)} %convert_element_type.38, f32[512]{0:T(512)S(1)} %add_rsqrt_fusion, bf16[512,1024]{1,0:T(8,128)(2,1)} %all-gather.3.cloned.1.call-done, f32[512]{0:T(512)S(1)} %add_divide_fusion), kind=kOutput, calls=%fused_computation.13 | convolution fusion | flops 4309123072 | bytes 13651968 | tf_op jit(solution)/shard_map/dot_general | solution.py:465
  63.2 135.3 %shard_map.129 = f32[64,4096]{1,0:T(8,128)S(1)} custom-call(bf16[4,2,2,64,4096]{4,3,2,1,0:T(8,128)(2,1)S(1)} %bitcast.21), custom_call_target="tpu_custom_call" | custom-call | flops 16777216 | bytes 33554432 | tf_op jit(solution)/shard_map/pallas_call | solution.py:390
  198.5 0.9 add_convert_fusion.tile_ref
  199.4 85.3 %shard_map.130 = bf16[16,64,4096]{2,1,0:T(8,128)(2,1)} custom-call(bf16[64,4096]{1,0:T(8,128)(2,1)} %add_convert_fusion.tile_ref), custom_call_target="tpu_custom_call" | custom-call | bytes 16777216 | tf_op jit(solution)/shard_map/pallas_call | solution.py:200
  284.7 4.1 %gather_fusion = bf16[4,64,4096]{2,1,0:T(8,128)(2,1)S(1)} fusion(bf16[16,64,4096]{2,1,0:T(8,128)(2,1)} %shard_map.130, s32[1024]{0:T(1024)S(1)} %pad_clamp_fusion), kind=kCustom, calls=%fused_computation | custom fusion | bytes 4194320 | tf_op jit(solution)/shard_map/jit(_take)/gather | solution.py:479
  288.8 11.1 %fusion.11 = (f32[256,4096]{1,0:T(8,128)}, f32[256,4096]{1,0:T(8,128)}, f32[256,4096]{1,0:T(8,128)}) fusion(f32[256,4096]{1,0:T(8,128)} %param.19, pred[256]{0:T(512)(128)(4,1)S(1)} %broadcast_in_dim.63, bf16[4,64,4096]{2,1,0:T(8,128)(2,1)S(1)} %gather_fusion, pred[256]{0:T(512)(128)(4,1)S(1)} %broadcast_in_dim.68, f32[256,4096]{1,0:T(8,128)} %param.17, ...), kind=kLoop, calls=%fused_computation.19 | loop fusion | flops 18874368 | bytes 27263488 | tf_op jit(solution)/shard_map/jit(_where)/select_n | solution.py:492
  299.9 11.0 %fusion.8 = (f32[512]{0:T(512)S(1)}, f32[512,4096]{1,0:T(8,128)}) fusion(bf16[512,4096]{1,0:T(8,128)(2,1)} %param.10, f32[4096]{0:T(1024)S(1)} %convert_element_type.38, bf16[512,1024]{1,0:T(8,128)(2,1)S(1)} %copy-done.1, bf16[1024,4096]{1,0:T(8,128)(2,1)} %all-gather.5.cloned.1.call-done), kind=kOutput, calls=%fused_computation.12 | convolution fusion | flops 4303355392 | bytes 22038528 | tf_op jit(solution)/shard_map/dot_general | solution.py:472
  310.9 2.4 psum.23
  313.4 7.4 %fusion.6 = bf16[512,4096]{1,0:T(8,128)(2,1)} fusion(bf16[512,4096]{1,0:T(8,128)(2,1)} %param.10, f32[512,4096]{1,0:T(8,128)} %get-tuple-element.12, f32[512]{0:T(512)S(1)} %broadcast_multiply_fusion, f32[4096]{0:T(1024)S(1)} %convert_element_type.38, f32[512]{0:T(512)S(1)} %add_rsqrt_fusion), kind=kLoop, calls=%fused_computation.10 | loop fusion | flops 18874368 | bytes 16797696 | tf_op jit(solution)/shard_map/convert_element_type | solution.py:478
  (28 shorter events, 0.6 us)
Async XLA Ops:
  7.2 34.2 %all-reduce.2.cloned.1.call-start = ((), (), s32[]{:S(2)}) async-start(), calls=%async_computation.1 | async-start | bytes 2097152 | tf_op jit(solution)/shard_map/psum | solution.py:451
  13.5 8.5 %copy-start.3 = (s32[16]{0:T(128)S(1)}, s32[16]{0:T(128)}, u32[]{:S(2)}) copy-start(s32[16]{0:T(128)} %param.16) | copy-start | bytes 196
  13.5 15.1 %copy-start.4 = (s32[16]{0:T(128)S(1)}, s32[16]{0:T(128)}, u32[]{:S(2)}) copy-start(s32[16]{0:T(128)} %param.15) | copy-start | bytes 196
  13.5 39.8 %copy-start.2 = (s32[512]{0:T(512)S(1)}, s32[512]{0:T(512)}, u32[]{:S(2)}) copy-start(s32[512]{0:T(512)} %param.14) | copy-start | bytes 6148
  20.4 32.8 %all-gather.3.cloned.1.call-start = ((), (), s32[]{:S(2)}) async-start(), calls=%async_computation | async-start | bytes 1572864 | tf_op jit(solution)/shard_map/all_gather | solution.py:447
  21.2 278.7 %all-gather.5.cloned.1.call-start = ((), (), s32[]{:S(2)}) async-start(), calls=%async_computation.2 | async-start | bytes 8912896 | tf_op jit(solution)/shard_map/all_gather | solution.py:446
  53.2 3.5 %copy-start = (bf16[512,4096]{1,0:T(8,128)(2,1)S(1)}, bf16[512,4096]{1,0:T(8,128)(2,1)}, u32[]{:S(2)}) copy-start(bf16[512,4096]{1,0:T(8,128)(2,1)} %param.10) | copy-start | bytes 12582916
  288.8 11.1 %copy-start.1 = (bf16[512,1024]{1,0:T(8,128)(2,1)S(1)}, bf16[512,1024]{1,0:T(8,128)(2,1)}, u32[]{:S(2)}) copy-start(bf16[512,1024]{1,0:T(8,128)(2,1)} %all-gather.3.cloned.1.call-done) | copy-start | bytes 3145732
Sparse Core Ops, SparseCore 0:
  20.5 20.7 all-reduce.1
  43.0 10.1 all-gather.2
  56.4 150.8 all-gather.4

commit v2 on v1

--- a/solution.py
+++ b/solution.py
@@ -47,6 +47,8 @@
         self.planes = planes
         me = lax.axis_index("dp")
         self.mp = lax.axis_index("mp")
+        self.me = me
+        self.cores = lax.axis_size("mp")
         self.line = me // PLANE
         self.row = (me // 2) % 2
         self.col = me % 2
@@ -72,7 +74,21 @@
     def has_below(self):
         return self.line > 0
 
-    def greet(self):
+    def core_peer(self, step):
+        return (self.me, (self.mp + step) % self.cores)
+
+    def greet_cores(self):
+        barrier = pltpu.get_barrier_semaphore()
+        for step in range(1, self.cores):
+            pl.semaphore_signal(
+                barrier,
+                inc=1,
+                device_id=self.core_peer(step),
+                device_id_type=pl.DeviceIdType.MESH,
+            )
+        pl.semaphore_wait(barrier, self.cores - 1)
+
+    def greet(self, with_cores=False):
         barrier = pltpu.get_barrier_semaphore()
         mesh_ids = pl.DeviceIdType.MESH
         for peer in (self.col_peer(), self.row_peer()):
@@ -87,7 +103,14 @@
             pl.semaphore_signal(barrier, inc=1, device_id=self.below(), device_id_type=mesh_ids)
 
         ends = jnp.where(self.line > 0, 1, 0) + jnp.where(self.line + 1 < self.planes, 1, 0)
-        pl.semaphore_wait(barrier, 2 + ends)
+        others = 0
+        if with_cores:
+            others = self.cores - 1
+            for step in range(1, self.cores):
+                pl.semaphore_signal(
+                    barrier, inc=1, device_id=self.core_peer(step), device_id_type=mesh_ids
+                )
+        pl.semaphore_wait(barrier, 2 + others + ends)
 
 
 def remote(src, dst, send_sem, recv_sem, peer):
@@ -101,13 +124,194 @@
     )
 
 
-def gather_kernel(planes, tile_ref, out_ref, own_sem, send_sems, recv_sems):
+def clip_kernel(
+    normed_ref, cot_ref, doc_col_ref, doc_row_ref, full_ref, clipped_ref, grams, send_sems, recv_sems
+):
+    links = Links(1)
+    me, cores = links.mp, links.cores
+    tokens, width = cot_ref.shape
+    block = tokens // 2
+    links.greet_cores()
+
+    def cot_slot(core):
+        return full_ref.at[:, pl.ds(pl.multiple_of(core * width, width), width)]
+
+    def cot_copy(core, step):
+        return remote(
+            cot_ref,
+            cot_slot(core),
+            send_sems.at[step - 1, 0],
+            recv_sems.at[core, 0],
+            links.core_peer(step),
+        )
+
+    def gram_copy(core, step, part):
+        rows = pl.ds(part * block, block)
+        return remote(
+            grams.at[core, rows],
+            grams.at[core, rows],
+            send_sems.at[step - 1, 1 + part],
+            recv_sems.at[core, 1 + part],
+            links.core_peer(step),
+        )
+
+    steps = range(1, cores)
+    for step in steps:
+        cot_copy(me, step).start()
+    full_ref[:, pl.ds(pl.multiple_of(me * width, width), width)] = cot_ref[...]
+    for part in range(2):
+        grams[me, pl.ds(part * block, block), :] = lax.dot_general(
+            normed_ref[pl.ds(part * block, block), :],
+            normed_ref[...],
+            (((1,), (1,)), ((), ())),
+            preferred_element_type=jnp.float32,
+        )
+        for step in steps:
+            gram_copy(me, step, part).start()
+    for step in steps:
+        cot_copy((me + step) % cores, step).wait_recv()
+    gram_values = lax.dot_general(
+        full_ref[...],
+        full_ref[...],
+        (((1,), (1,)), ((), ())),
+        preferred_element_type=jnp.float32,
+    )
+    same_doc = doc_col_ref[...] == doc_row_ref[...]
+    for step in steps:
+        for part in range(2):
+            gram_copy((me + step) % cores, step, part).wait_recv()
+    gram_features = grams[0]
+    for core in range(1, cores):
+        gram_features = gram_features + grams[core]
+    product = jnp.where(same_doc, gram_features * gram_values, 0.0)
+    row_sums = jnp.sum(product, axis=0, keepdims=True)
+    squared = jnp.sum(jnp.where(same_doc, row_sums, 0.0), axis=1, keepdims=True)
+    scales = CLIP_NORM / (jnp.sqrt(squared) + 0.01)
+    clipped_ref[...] = (full_ref[...].astype(jnp.float32) * scales).astype(jnp.bfloat16)
+    for step in steps:
+        cot_copy(me, step).wait_send()
+        for part in range(2):
+            gram_copy(me, step, part).wait_send()
+
+
+def clip_by_document(normed, cot, doc_ids):
+    tokens, width = cot.shape
+    cores = lax.axis_size("mp")
+    vmem = pl.BlockSpec(memory_space=pltpu.VMEM)
+    full = jax.ShapeDtypeStruct((tokens, width * cores), cot.dtype)
+    return pl.pallas_call(
+        clip_kernel,
+        out_shape=(full, full),
+        in_specs=[vmem] * 4,
+        out_specs=(vmem, vmem),
+        scratch_shapes=[
+            pltpu.VMEM((cores, tokens, tokens), jnp.float32),
+            pltpu.SemaphoreType.DMA((cores - 1, 3)),
+            pltpu.SemaphoreType.DMA((cores, 3)),
+        ],
+        compiler_params=pltpu.CompilerParams(
+            collective_id=3, has_side_effects=True, vmem_limit_bytes=40 * 1024 * 1024
+        ),
+        cost_estimate=pl.CostEstimate(
+            flops=2 * tokens * tokens * (normed.shape[1] + width * cores),
+            bytes_accessed=2 * tokens * (normed.shape[1] + 4 * width * cores),
+            transcendentals=0,
+        ),
+    )(normed, cot, doc_ids[:, None], doc_ids[None, :])
+
+
+def gather_kernel(
+    planes,
+    tile_ref,
+    weight_hbm,
+    cot_ref,
+    input_ref,
+    gain_ref,
+    inv_ref,
+    out_ref,
+    grad_ref,
+    weight_ref,
+    weighted_ref,
+    inner_ref,
+    own_sem,
+    weight_sem,
+    send_sems,
+    recv_sems,
+    inner_send,
+    inner_recv,
+):
     links = Links(planes)
+    core, cores = links.mp, links.cores
+    width = input_ref.shape[1]
+    tile = width // 8
+    fetch = pltpu.make_async_copy(weight_hbm, weight_ref, weight_sem)
+    fetch.start()
     half = tile_ref.shape[1] // 2
     mine = links.index(links.line, links.row, links.col)
     own = pltpu.make_async_copy(tile_ref, out_ref.at[mine], own_sem)
     own.start()
-    links.greet()
+    links.greet(True)
+
+    def inner_copy(slot, step):
+        return remote(
+            inner_ref.at[slot],
+            inner_ref.at[slot],
+            inner_send.at[step - 1],
+            inner_recv.at[slot],
+            links.core_peer(step),
+        )
+
+    def project(low, high):
+        def at(index, carry):
+            columns = pl.ds(pl.multiple_of(index * tile, tile), tile)
+            weighted = gain_ref[:, columns] * jnp.dot(
+                cot_ref[...], weight_ref[:, columns], preferred_element_type=jnp.float32
+            )
+            weighted_ref[:, columns] = weighted
+            product = weighted * input_ref[:, columns].astype(jnp.float32)
+            total = inner_ref[core]
+            for lane in range(tile // 128):
+                total = total + product[:, lane * 128 : (lane + 1) * 128]
+            inner_ref[core] = total
+            return carry
+
+        lax.fori_loop(low, high, at, 0)
+
+    def project_first():
+        inner_ref[core] = jnp.zeros(inner_ref.shape[1:], jnp.float32)
+        fetch.wait()
+        project(0, 4)
+
+    def project_rest():
+        project(4, 8)
+        for step in range(1, cores):
+            inner_copy(core, step).start()
+
+    def inner_done():
+        for step in range(1, cores):
+            inner_copy((core + step) % cores, step).wait_recv()
+        total = inner_ref[0]
+        for slot in range(1, cores):
+            total = total + inner_ref[slot]
+        inner = jnp.sum(total, axis=1, keepdims=True) / (width * cores)
+        inv = inv_ref[...]
+        factor = inv * inv * inv * inner
+
+        def at(index, carry):
+            columns = pl.ds(pl.multiple_of(index * tile, tile), tile)
+            grad_ref[:, columns] = (
+                inv * weighted_ref[:, columns] - input_ref[:, columns].astype(jnp.float32) * factor
+            ).astype(jnp.bfloat16)
+            return carry
+
+        lax.fori_loop(0, 8, at, 0)
+
+    chores = [project_first, project_rest, inner_done]
+
+    def chore():
+        if chores:
+            chores.pop(0)()
+
     ways = (links.col_peer(), links.row_peer(), links.above(), links.below())
     pending = []
 
@@ -161,6 +365,7 @@
         start(mine, part, 2, links.has_above(), True)
         start(mine, part, 3, links.has_below(), True)
     spread(links.line, None, True)
+    chore()
     lines = [[(links.line, None)]]
     for step in range(1, planes):
         from_below = links.line - step
@@ -178,9 +383,12 @@
         spread(from_above, got_above, False)
         for line, guard in lines[-1]:
             relay(line, guard)
+        chore()
         lines.append([(from_below, got_below), (from_above, got_above)])
     for line, guard in lines[-1]:
         relay(line, guard)
+    while chores:
+        chore()
     for group in lines:
         for line, guard in group:
             for part in (0, 1):
@@ -193,31 +401,54 @@
         else:
             pl.when(guard)(copy.wait_send)
     own.wait()
-
-
-def gather_tiles(tile, count):
+    for step in range(1, cores):
+        inner_copy(core, step).wait_send()
+
+
+def gather_tiles(tile, count, full_weight, full_cot, layer_input, gain_row, inv_rms):
     rows, width = tile.shape
+    tokens = layer_input.shape[0]
+    cores = lax.axis_size("mp")
+    vmem = pl.BlockSpec(memory_space=pltpu.VMEM)
+    anywhere = pl.BlockSpec(memory_space=pl.ANY)
     return pl.pallas_call(
         functools.partial(gather_kernel, count // PLANE),
-        out_shape=jax.ShapeDtypeStruct((count, rows, width), tile.dtype),
-        in_specs=[pl.BlockSpec(memory_space=pl.ANY)],
-        out_specs=pl.BlockSpec(memory_space=pl.ANY),
+        out_shape=(
+            jax.ShapeDtypeStruct((count, rows, width), tile.dtype),
+            jax.ShapeDtypeStruct((tokens, width), jnp.bfloat16),
+        ),
+        in_specs=[anywhere, anywhere, vmem, vmem, vmem, vmem],
+        out_specs=(anywhere, vmem),
         scratch_shapes=[
+            pltpu.VMEM(full_weight.shape, full_weight.dtype),
+            pltpu.VMEM((tokens, width), jnp.float32),
+            pltpu.VMEM((cores, tokens, 128), jnp.float32),
+            pltpu.SemaphoreType.DMA,
             pltpu.SemaphoreType.DMA,
             pltpu.SemaphoreType.DMA((count, 2, 4)),
             pltpu.SemaphoreType.DMA((count, 2)),
+            pltpu.SemaphoreType.DMA((cores - 1,)),
+            pltpu.SemaphoreType.DMA((cores,)),
         ],
-        compiler_params=pltpu.CompilerParams(collective_id=1, has_side_effects=True),
+        compiler_params=pltpu.CompilerParams(
+            collective_id=1, has_side_effects=True, vmem_limit_bytes=48 * 1024 * 1024
+        ),
         cost_estimate=pl.CostEstimate(
-            flops=0, bytes_accessed=2 * count * rows * width * 2, transcendentals=0
+            flops=2 * tokens * width * full_weight.shape[0],
+            bytes_accessed=6 * count * rows * width,
+            transcendentals=0,
         ),
-    )(tile)
+    )(tile, full_weight, full_cot, layer_input, gain_row, inv_rms)
 
 
 def scatter_kernel(
     planes,
+    clipped_ref,
+    normed_ref,
+    seed_ref,
+    out_ref,
     part_ref,
-    out_ref,
+    total_ref,
     first_in,
     second_in,
     line_in,
@@ -273,6 +504,45 @@
             links.above() if side == 0 else links.below(),
         )
 
+    def make_tiles(line):
+        plane_rows = PLANE * rows
+        tile = width // 8
+
+        def at(index, carry):
+            span = pl.ds(pl.multiple_of(index * tile, tile), tile)
+            product = lax.dot_general(
+                clipped_ref[:, line * plane_rows : (line + 1) * plane_rows],
+                normed_ref[:, span],
+                (((0,), (0,)), ((), ())),
+                preferred_element_type=jnp.float32,
+            )
+            for lane in range(PLANE):
+                part_ref[line, lane // 2, lane % 2, :, span] = product[
+                    lane * rows : (lane + 1) * rows
+                ].astype(jnp.bfloat16)
+            return carry
+
+        lax.fori_loop(0, 8, at, 0)
+
+    def draw_noise():
+        seed = seed_ref[0]
+        tile = width // 8
+        full_width = width * links.cores
+        deep = 8
+
+        def at(index, carry):
+            top = pl.multiple_of((index // 8) * deep, deep)
+            left = pl.multiple_of((index % 8) * tile, tile)
+            row_pos = top + lax.broadcasted_iota(jnp.int32, (deep, tile), 0)
+            col_pos = (
+                links.mp * width + left + lax.broadcasted_iota(jnp.int32, (deep, tile), 1)
+            )
+            noise = gauss_noise(seed, row_pos * full_width + col_pos)
+            total_ref[pl.ds(top, deep), pl.ds(left, tile)] = NOISE_MULT * CLIP_NORM * noise
+            return carry
+
+        lax.fori_loop(0, (rows // deep) * 8, at, 0)
+
     def send_first(line):
         for part in (0, 1):
             copy = first_copy(line, part)
@@ -318,7 +588,7 @@
             @pl.when(place == line)
             def _():
                 def step(at):
-                    out_ref[at, columns(part)] = plane_sum(line, part, at)
+                    total_ref[at, columns(part)] += plane_sum(line, part, at)
 
                 by_blocks(step)
 
@@ -352,10 +622,13 @@
 
     ahead = 2
     for line in order[:ahead]:
+        make_tiles(line)
         send_first(line)
+    draw_noise()
     for index, line in enumerate(order):
         send_second(line)
         if index + ahead < planes:
+            make_tiles(order[index + ahead])
             send_first(order[index + ahead])
         if index > 0:
             send_line(order[index - 1])
@@ -369,12 +642,16 @@
                 line_copy(place, part, side).wait_recv()
 
                 def step(at):
-                    out_ref[at, columns(part)] += line_in[side, place, part, at, :].astype(
+                    total_ref[at, columns(part)] += line_in[side, place, part, at, :].astype(
                         jnp.float32
                     )
 
                 by_blocks(step)
 
+    def finish(at):
+        out_ref[at, :] = total_ref[at, :].astype(jnp.bfloat16)
+
+    by_blocks(finish)
     for guard, copy in pending:
         if guard is None:
             copy.wait_send()
@@ -382,17 +659,20 @@
             pl.when(guard)(copy.wait_send)
 
 
-def scatter_sum(partial_tiles, count):
+def scatter_sum(clipped, normed, seed, count):
     planes = count // PLANE
-    rows = partial_tiles.shape[0] // count
-    width = partial_tiles.shape[1]
+    rows = clipped.shape[1] // count
+    width = normed.shape[1]
+    vmem = pl.BlockSpec(memory_space=pltpu.VMEM)
     half = width // 2
     return pl.pallas_call(
         functools.partial(scatter_kernel, planes),
-        out_shape=jax.ShapeDtypeStruct((rows, width), jnp.float32),
-        in_specs=[pl.BlockSpec(memory_space=pltpu.VMEM)],
-        out_specs=pl.BlockSpec(memory_space=pltpu.VMEM),
+        out_shape=jax.ShapeDtypeStruct((rows, width), jnp.bfloat16),
+        in_specs=[vmem, vmem, pl.BlockSpec(memory_space=pltpu.SMEM)],
+        out_specs=vmem,
         scratch_shapes=[
+            pltpu.VMEM((planes, 2, 2, rows, width), jnp.bfloat16),
+            pltpu.VMEM((rows, width), jnp.float32),
             pltpu.VMEM((planes, 2, 2, rows, half), jnp.bfloat16),
             pltpu.VMEM((planes, 2, rows, half), jnp.bfloat16),
             pltpu.VMEM((2, planes, 2, rows, half), jnp.bfloat16),
@@ -407,11 +687,11 @@
             collective_id=2, has_side_effects=True, vmem_limit_bytes=40 * 1024 * 1024
         ),
         cost_estimate=pl.CostEstimate(
-            flops=4 * count * rows * width,
+            flops=2 * count * rows * width * clipped.shape[0],
             bytes_accessed=8 * count * rows * width,
             transcendentals=0,
         ),
-    )(partial_tiles.reshape(planes, 2, 2, rows, width))
+    )(clipped, normed, seed)
 
 
 def body(
@@ -432,27 +712,14 @@
     slot_count = master.shape[0] // group_rows
     cycle_size = lax.axis_size("dp")
     my_group = lax.axis_index("dp")
-    my_column = lax.axis_index("mp")
     inputs = layer_input.astype(jnp.float32)
     gain_row = norm_gain.astype(jnp.float32)
     squares = lax.psum(jnp.sum(inputs * inputs, axis=1), "mp")
     inv_rms = lax.rsqrt(squares / full_width + EPS_NORM)[:, None]
     normed = (inputs * inv_rms * gain_row).astype(jnp.bfloat16)
     seed_value = noise_seeds[my_group]
-    row_pos = jnp.arange(group_rows, dtype=jnp.int32)[:, None]
-    col_pos = my_column * part_width + jnp.arange(part_width, dtype=jnp.int32)[None, :]
-    positions = row_pos * full_width + col_pos
-    noise = lax.optimization_barrier(NOISE_MULT * CLIP_NORM * gauss_noise(seed_value, positions))
     full_weight = lax.all_gather(value_weight, "dp", axis=0, tiled=True)
-    full_cot = lax.all_gather(value_cotangent, "mp", axis=1, tiled=True)
-    same_doc = (doc_ids[:, None] == doc_ids[None, :]).astype(jnp.float32)
-    gram_part = jnp.dot(normed, normed.T, preferred_element_type=jnp.float32)
-    gram_values = jnp.dot(full_cot, full_cot.T, preferred_element_type=jnp.float32)
-    gram_features = lax.psum(gram_part, "mp")
-    mine_sums = jnp.sum(same_doc * gram_features * gram_values, axis=1)
-    squared = jnp.dot(same_doc, mine_sums, precision=lax.Precision.HIGHEST)
-    scales = CLIP_NORM / (jnp.sqrt(squared) + 0.01)
-    clipped = (full_cot.astype(jnp.float32) * scales[:, None]).astype(jnp.bfloat16)
+    full_cot, clipped = clip_by_document(normed, value_cotangent, doc_ids)
     group_ids = jnp.arange(cycle_size, dtype=jnp.int32)
     earlier = group_ids[:, None] > group_ids[None, :]
     same_owner = owners[:, None] == owners[None, :]
@@ -462,20 +729,10 @@
     sources = jnp.sum(jnp.where(holds_slot, group_ids[None, :], 0), axis=1)
     filled = jnp.any(holds_slot, axis=1)
     filled_rows = jnp.repeat(filled, group_rows)
-    partial_grad = lax.dot_general(
-        clipped, normed, (((0,), (0,)), ((), ())), preferred_element_type=jnp.float32
-    ).astype(jnp.bfloat16)
-    grad_tile = scatter_sum(partial_grad, cycle_size)
-    noisy_tile = (grad_tile + noise).astype(jnp.bfloat16)
-    arrived = gather_tiles(noisy_tile, cycle_size)
-    late_cot, arrived = lax.optimization_barrier((full_cot, arrived))
-    dnormed = jnp.dot(late_cot, full_weight, preferred_element_type=jnp.float32)
-    weighted = gain_row * dnormed
-    inner_sum = lax.psum(jnp.sum(weighted * inputs, axis=1), "mp")
-    input_grad = (
-        inv_rms * weighted
-        - inputs * inv_rms * inv_rms * inv_rms * (inner_sum / full_width)[:, None]
-    ).astype(jnp.bfloat16)
+    noisy_tile = scatter_sum(clipped, normed, seed_value[None], cycle_size)
+    arrived, input_grad = gather_tiles(
+        noisy_tile, cycle_size, full_weight, full_cot, layer_input, gain_row[None, :], inv_rms
+    )
     gathered = jnp.take(arrived, sources, axis=0).reshape(slot_count * group_rows, part_width)
     gathered = gathered.astype(jnp.float32)
     first_new = BETA_ONE * moment_one + (1.0 - BETA_ONE) * gathered

time: 331 us -> 278 us (0.84)
  matrix products: 27.9 us -> 0 us
  waiting for transfers between devices: 25.1 us -> 11.5 us
  other arithmetic: 29.7 us -> 19.3 us
  local copies, waits for them, and re-layouts: 5 us -> 9.99 us
  Pallas kernels: 221 us -> 217 us
    dot_general x5 -> x0, matrix products: 27.9 us -> none  [the longest x1 11 us: body(): dnormed = jnp.dot(late_cot, full_weight, preferred_element_type=jnp.float32)]
    psum x1 -> x0, waiting for transfers between devices: 12.1 us -> none  [body(): gram_features = lax.psum(gram_part, 'mp')]
    all_gather x1 -> x0, waiting for transfers between devices: 11.9 us -> none  [body(): full_cot = lax.all_gather(value_cotangent, 'mp', axis=1, tiled=True)]
    all_gather x1, waiting for transfers between devices: 0.01 us -> 10.9 us  [body(): full_weight = lax.all_gather(value_weight, 'dp', axis=0, tiled=True)]
    pallas_call x1, Pallas kernels: 135 us -> 127 us  [scatter_sum(): pl.pallas_call(functools.partial(scatter_kernel, planes), out_shape=jax.S...]
    mul x2 -> x0, other arithmetic: 5.99 us -> none  [the longest x1 5.99 us: body(): NOISE_MULT * CLIP_NORM * gauss_noise(seed_value, positions)]
    pallas_call x0 -> x1, Pallas kernels: none -> 5.24 us  [clip_by_document(): pl.pallas_call(clip_kernel, out_shape=(full, full), in_specs=[vmem] * 4,...]
    convert_element_type x2 -> x1, other arithmetic: 8.32 us -> 3.88 us  [body(): normed = (inputs * inv_rms * gain_row).astype(jnp.bfloat16)]
  transfers between devices with their start and end apart: 3 -> 1, of which waited for: 2 -> 1; matrix products, arithmetic and copies ran while one was open for 10% -> 4% of each run, Pallas kernels for 67% -> 48%
where the time goes in v2:
time: 278 us; the launch traced here: 274 us
  Pallas kernels  217 us (78%)
  other arithmetic  19.3 us (7%)
  between operations  14.2 us (5%)
  waiting for transfers between devices  11.5 us (4%)
  local copies, waits for them, and re-layouts  9.99 us (4%)
    pallas_call x1, Pallas kernels, scatter_sum(): pl.pallas_call(functools.partial(scatter_kernel, planes), out_shape=jax.S...  127 us
    pallas_call x1, Pallas kernels, gather_tiles(): pl.pallas_call(functools.partial(gather_kernel, count // PLANE), out_shap...  84.4 us
    select_n x1, other arithmetic, body(): new_moment_two = jnp.where(keep_mask, second_new, moment_two)  11.2 us
    all_gather x1, waiting for transfers between devices, body(): full_weight = lax.all_gather(value_weight, 'dp', axis=0, tiled=True)  10.9 us
  transfers between devices with their start and end apart: 1, of which 1 were waited for; matrix products, arithmetic and copies ran while one was open for 4% of the time, Pallas kernels for 48%

profile of v2, /device:TPU:28, one launch (start us, length us, event | category | flops | bytes accessed | tf_op | source)
XLA Modules:
  0.0 274.3 jit_solution(16261987506432405393)
XLA Ops:
  7.2 0.0 all-gather.2.cloned.1.call-start
  7.2 0.7 all-gather.2.cloned.1.call-update
  7.9 0.7 convert_element_type.16
  8.6 0.8 copy.16.doc_col_ref
  9.5 3.1 %fusion = f32[512]{0:T(512)S(1)} fusion(bf16[512,4096]{1,0:T(8,128)(2,1)} %input_ref.1), kind=kLoop, calls=%fused_computation.3 | loop fusion | flops 6290944 | bytes 4196352 | tf_op jit(solution)/shard_map/reduce_sum | solution.py:717
  12.5 2.5 psum.7
  15.0 0.2 copy.17.inv_ref
  15.2 0.2 convert_reduce_fusion
  15.4 0.1 select_reduce_fusion
  15.5 0.1 broadcast_in_dim.75
  15.6 0.1 broadcast_in_dim.76
  15.7 0.1 fusion.9
  15.8 0.1 broadcast_in_dim.70
  15.9 0.1 broadcast_in_dim.71
  16.0 0.6 dynamic_slice.3.seed_ref
  16.6 3.9 %fusion.2.normed_ref = bf16[512,4096]{1,0:T(8,128)(2,1)S(1)} fusion(bf16[512,4096]{1,0:T(8,128)(2,1)} %input_ref.1, f32[4096]{0:T(1024)S(1)} %convert_element_type.16, f32[512]{0:T(512)S(1)} %add_rsqrt_fusion), kind=kLoop, calls=%fused_computation.5 | loop fusion | flops 8388608 | bytes 8407040 | tf_op jit(solution)/shard_map/convert_element_type | solution.py:719
  20.5 5.2 %shard_map.129 = (bf16[512,1024]{1,0:T(8,128)(2,1)S(1)}, bf16[512,1024]{1,0:T(8,128)(2,1)S(1)}) custom-call(bf16[512,4096]{1,0:T(8,128)(2,1)S(1)} %fusion.2.normed_ref, bf16[512,512]{1,0:T(8,128)(2,1)S(1)} %copy-done.3, s32[512,1]{1,0:T(8,128)S(1)} %copy.16.doc_col_ref, s32[1,512]{1,0:T(1,128)S(1)} %bitcast.18), custom_call_target="tpu_custom_call" | custom-call | flops 2684354560 | bytes 8388608 | tf_op jit(solution)/shard_map/pallas_call | solution.py:202
  25.7 127.2 %shard_map.130.tile_ref = bf16[64,4096]{1,0:T(8,128)(2,1)S(1)} custom-call(bf16[512,1024]{1,0:T(8,128)(2,1)S(1)} %get-tuple-element.8.clipped_ref, bf16[512,4096]{1,0:T(8,128)(2,1)S(1)} %fusion.2.normed_ref, s32[1]{0:T(128)} %dynamic_slice.3.seed_ref), custom_call_target="tpu_custom_call" | custom-call | flops 4294967296 | bytes 33554432 | tf_op jit(solution)/shard_map/pallas_call | solution.py:668
  152.9 10.9 %all-gather.2.cloned.1.call-done.weight_hbm = bf16[1024,4096]{1,0:T(8,128)(2,1)} async-done(((bf16[64,4096]{1,0:T(8,128)(2,1)}), bf16[1024,4096]{1,0:T(8,128)(2,1)}) %all-gather.2.cloned.1.call-update) | async-done | bytes 8388624 | tf_op jit(solution)/shard_map/all_gather | solution.py:721
  163.8 84.4 %shard_map.131 = (bf16[16,64,4096]{2,1,0:T(8,128)(2,1)}, bf16[512,4096]{1,0:T(8,128)(2,1)S(1)}) custom-call(bf16[64,4096]{1,0:T(8,128)(2,1)S(1)} %shard_map.130.tile_ref, bf16[1024,4096]{1,0:T(8,128)(2,1)} %all-gather.2.cloned.1.call-done.weight_hbm, bf16[512,1024]{1,0:T(8,128)(2,1)S(1)} %get-tuple-element.9.cot_ref, bf16[512,4096]{1,0:T(8,128)(2,1)} %input_ref.1, ...), custom_call_target="tpu_custom_call" | custom-call | flops 4294967296 | bytes 25165824 | tf_op jit(solution)/shard_map/pallas_call | solution.py:414
  248.2 2.0 copy-done
  250.2 4.1 %gather_fusion = bf16[4,64,4096]{2,1,0:T(8,128)(2,1)S(1)} fusion(bf16[16,64,4096]{2,1,0:T(8,128)(2,1)} %get-tuple-element.11, s32[1024]{0:T(1024)S(1)} %pad_clamp_fusion), kind=kCustom, calls=%fused_computation | custom fusion | bytes 4194320 | tf_op jit(solution)/shard_map/jit(_take)/gather | solution.py:736
  254.3 11.2 %fusion.5 = (f32[256,4096]{1,0:T(8,128)}, f32[256,4096]{1,0:T(8,128)}, f32[256,4096]{1,0:T(8,128)}) fusion(f32[256,4096]{1,0:T(8,128)} %param.19, pred[256]{0:T(512)(128)(4,1)S(1)} %broadcast_in_dim.71, bf16[4,64,4096]{2,1,0:T(8,128)(2,1)S(1)} %gather_fusion, pred[256]{0:T(512)(128)(4,1)S(1)} %broadcast_in_dim.76, f32[256,4096]{1,0:T(8,128)} %param.17, ...), kind=kLoop, calls=%fused_computation.11 | loop fusion | flops 18874368 | bytes 27263488 | tf_op jit(solution)/shard_map/jit(_where)/select_n | solution.py:749
  265.4 2.0 copy.19
  (16 shorter events, 0.1 us)
Async XLA Ops:
  7.2 8.0 %copy-start.4 = (s32[16]{0:T(128)S(1)}, s32[16]{0:T(128)}, u32[]{:S(2)}) copy-start(s32[16]{0:T(128)} %param.15) | copy-start | bytes 196
  7.2 8.8 %copy-start.5 = (s32[16]{0:T(128)S(1)}, s32[16]{0:T(128)}, u32[]{:S(2)}) copy-start(s32[16]{0:T(128)} %param.16) | copy-start | bytes 196
  7.2 156.6 %all-gather.2.cloned.1.call-start = ((), (), s32[]{:S(2)}) async-start(), calls=%async_computation | async-start | bytes 8912896 | tf_op jit(solution)/shard_map/all_gather | solution.py:721
  16.6 3.9 %copy-start.2 = (s32[512]{0:T(512)S(1)}, s32[512]{0:T(512)}, u32[]{:S(2)}) copy-start(s32[512]{0:T(512)} %param.14) | copy-start | bytes 6148
  16.6 3.9 %copy-start.3 = (bf16[512,512]{1,0:T(8,128)(2,1)S(1)}, bf16[512,512]{1,0:T(8,128)(2,1)}, u32[]{:S(2)}) copy-start(bf16[512,512]{1,0:T(8,128)(2,1)} %cot_ref.1) | copy-start | bytes 1572868
  248.2 2.0 copy-start
  254.3 11.2 %copy-start.1 = (bf16[512,4096]{1,0:T(8,128)(2,1)S(1)}, bf16[512,4096]{1,0:T(8,128)(2,1)}, u32[]{:S(2)}) copy-start(bf16[512,4096]{1,0:T(8,128)(2,1)} %copy-done) | copy-start | bytes 12582916
Sparse Core Ops, SparseCore 0:
  10.8 152.9 all-gather.1

commit v3 on v2

--- a/solution.py
+++ b/solution.py
@@ -77,17 +77,6 @@
     def core_peer(self, step):
         return (self.me, (self.mp + step) % self.cores)
 
-    def greet_cores(self):
-        barrier = pltpu.get_barrier_semaphore()
-        for step in range(1, self.cores):
-            pl.semaphore_signal(
-                barrier,
-                inc=1,
-                device_id=self.core_peer(step),
-                device_id_type=pl.DeviceIdType.MESH,
-            )
-        pl.semaphore_wait(barrier, self.cores - 1)
-
     def greet(self, with_cores=False):
         barrier = pltpu.get_barrier_semaphore()
         mesh_ids = pl.DeviceIdType.MESH
@@ -124,17 +113,204 @@
     )
 
 
+def run_gather(links, planes, tile_ref, out_ref, own_sem, send_sems, recv_sems, chores):
+    width = tile_ref.shape[1]
+    extra = 2 * ((width // 128) * 3 // 32) * 128
+    half = (width - extra) // 2
+    spans = (pl.ds(0, half), pl.ds(half, half), pl.ds(2 * half, extra))
+    line, row, col = links.line, links.row, links.col
+    mine = links.index(line, row, col)
+    ways = (links.col_peer(), links.row_peer(), links.above(), links.below())
+    pending = []
+
+    def transfer(shard, part, way, from_tile=False):
+        target = out_ref.at[shard, :, spans[part]]
+        return remote(
+            tile_ref.at[:, spans[part]] if from_tile else target,
+            target,
+            send_sems.at[shard, part, way],
+            recv_sems.at[shard, part],
+            ways[way],
+        )
+
+    def start(shard, part, way, guard, from_tile=False):
+        copy = transfer(shard, part, way, from_tile)
+        pending.append((guard, copy))
+        if guard is None:
+            copy.start()
+        else:
+            pl.when(guard)(copy.start)
+
+    def arrive(shard, part, guard):
+        copy = transfer(shard, part, 0)
+        if guard is None:
+            copy.wait_recv()
+        else:
+            pl.when(guard)(copy.wait_recv)
+
+    def both(first, second):
+        return jnp.logical_and(first, second)
+
+    def chore():
+        if chores:
+            chores.pop(0)()
+
+    def spread(at, guard, from_tile):
+        shard = links.index(at, row, col)
+        start(shard, 0, 0, guard, from_tile)
+        start(shard, 1, 1, guard, from_tile)
+        start(shard, 0, 1, guard, from_tile)
+        start(shard, 1, 0, guard, from_tile)
+
+    def relay(at, guard):
+        shard = links.index(at, row, 1 - col)
+        arrive(shard, 0, guard)
+        start(shard, 0, 1, guard)
+        shard = links.index(at, 1 - row, col)
+        arrive(shard, 1, guard)
+        start(shard, 1, 0, guard)
+
+    def leave_plane():
+        for far_col in (col, 1 - col):
+            arrive(links.index(line, 1 - row, far_col), 2, None)
+        for at_row in (row, 1 - row):
+            for at_col in (col, 1 - col):
+                own = at_row is row and at_col is col
+                shard = links.index(line, at_row, at_col)
+                start(shard, 2, 2, links.has_above(), own)
+                start(shard, 2, 3, links.has_below(), own)
+
+    def carry(step):
+        for at, guard, way, onward in (
+            (line - step, line - step >= 0, 2, links.has_above()),
+            (line + step, line + step < planes, 3, links.has_below()),
+        ):
+            for lane in range(PLANE):
+                shard = at * PLANE + lane
+                arrive(shard, 2, guard)
+                start(shard, 2, way, both(guard, onward))
+
+    own = pltpu.make_async_copy(tile_ref, out_ref.at[mine], own_sem)
+    own.start()
+    for part in (0, 1):
+        start(mine, part, 2, links.has_above(), True)
+        start(mine, part, 3, links.has_below(), True)
+    if extra:
+        start(mine, 2, 0, None, True)
+        start(mine, 2, 1, None, True)
+    spread(line, None, True)
+    chore()
+    if extra:
+        shard = links.index(line, row, 1 - col)
+        arrive(shard, 2, None)
+        start(shard, 2, 1, None)
+    lines = [[(line, None)]]
+    carried = 0
+    for step in range(1, planes):
+        below, above = line - step, line + step
+        got_below, got_above = below >= 0, above < planes
+        for part in (0, 1):
+            shard = links.index(below, row, col)
+            arrive(shard, part, got_below)
+            start(shard, part, 2, both(got_below, links.has_above()))
+            shard = links.index(above, row, col)
+            arrive(shard, part, got_above)
+            start(shard, part, 3, both(got_above, links.has_below()))
+        spread(below, got_below, False)
+        spread(above, got_above, False)
+        if extra and step == min(2, planes - 1):
+            leave_plane()
+        if extra and step > 2:
+            carried += 1
+            carry(carried)
+        for at, guard in lines[-1]:
+            relay(at, guard)
+        chore()
+        lines.append([(below, got_below), (above, got_above)])
+    if extra and carried < planes - 1:
+        carried += 1
+        carry(carried)
+    for at, guard in lines[-1]:
+        relay(at, guard)
+    while chores:
+        chore()
+    if extra:
+        for step in range(carried + 1, planes):
+            carry(step)
+    for group in lines:
+        for at, guard in group:
+            for part in (0, 1):
+                arrive(links.index(at, 1 - row, 1 - col), part, guard)
+            arrive(links.index(at, 1 - row, col), 0, guard)
+            arrive(links.index(at, row, 1 - col), 1, guard)
+    for guard, copy in pending:
+        if guard is None:
+            copy.wait_send()
+        else:
+            pl.when(guard)(copy.wait_send)
+    own.wait()
+
+
+def gather_scratch(count):
+    return [
+        pltpu.SemaphoreType.DMA,
+        pltpu.SemaphoreType.DMA((count, 3, 4)),
+        pltpu.SemaphoreType.DMA((count, 3)),
+    ]
+
+
+def by_columns(width, step):
+    tile = width // 8
+
+    def at(index, carry):
+        step(pl.ds(pl.multiple_of(index * tile, tile), tile))
+        return carry
+
+    lax.fori_loop(0, 8, at, 0)
+
+
+def lane_sums(values):
+    total = values[:, :128]
+    for lane in range(1, values.shape[1] // 128):
+        total = total + values[:, lane * 128 : (lane + 1) * 128]
+    return total
+
+
 def clip_kernel(
-    normed_ref, cot_ref, doc_col_ref, doc_row_ref, full_ref, clipped_ref, grams, send_sems, recv_sems
+    planes,
+    tile_ref,
+    input_hbm,
+    gain_ref,
+    cot_ref,
+    doc_col_ref,
+    doc_row_ref,
+    weight_ref,
+    full_ref,
+    clipped_ref,
+    normed_ref,
+    inv_ref,
+    input_ref,
+    squares,
+    grams,
+    own_sem,
+    gather_send,
+    gather_recv,
+    input_sem,
+    send_sems,
+    recv_sems,
 ):
-    links = Links(1)
+    links = Links(planes)
     me, cores = links.mp, links.cores
-    tokens, width = cot_ref.shape
+    tokens, cot_width = cot_ref.shape
+    width = input_ref.shape[1]
     block = tokens // 2
-    links.greet_cores()
+    steps = range(1, cores)
+    fetch = pltpu.make_async_copy(input_hbm, input_ref, input_sem)
+    fetch.start()
+    links.greet(True)
 
     def cot_slot(core):
-        return full_ref.at[:, pl.ds(pl.multiple_of(core * width, width), width)]
+        return full_ref.at[:, pl.ds(pl.multiple_of(core * cot_width, cot_width), cot_width)]
 
     def cot_copy(core, step):
         return remote(
@@ -155,69 +331,128 @@
             links.core_peer(step),
         )
 
-    steps = range(1, cores)
-    for step in steps:
-        cot_copy(me, step).start()
-    full_ref[:, pl.ds(pl.multiple_of(me * width, width), width)] = cot_ref[...]
-    for part in range(2):
-        grams[me, pl.ds(part * block, block), :] = lax.dot_general(
-            normed_ref[pl.ds(part * block, block), :],
-            normed_ref[...],
+    def square_copy(core, step):
+        return remote(
+            squares.at[core],
+            squares.at[core],
+            send_sems.at[step - 1, 3],
+            recv_sems.at[core, 3],
+            links.core_peer(step),
+        )
+
+    def norm_and_grams():
+        for step in steps:
+            cot_copy(me, step).start()
+        fetch.wait()
+        squares[me] = jnp.zeros(squares.shape[1:], jnp.float32)
+
+        def square(columns):
+            values = input_ref[:, columns].astype(jnp.float32)
+            squares[me] = squares[me] + lane_sums(values * values)
+
+        by_columns(width, square)
+        for step in steps:
+            square_copy(me, step).start()
+        full_ref[:, pl.ds(pl.multiple_of(me * cot_width, cot_width), cot_width)] = cot_ref[...]
+        for step in steps:
+            square_copy((me + step) % cores, step).wait_recv()
+        total = squares[0]
+        for core in range(1, cores):
+            total = total + squares[core]
+        mean = jnp.sum(total, axis=1, keepdims=True) / (width * cores)
+        inv = lax.rsqrt(mean + EPS_NORM)
+        inv_ref[...] = inv
+
+        def norm(columns):
+            values = input_ref[:, columns].astype(jnp.float32)
+            normed_ref[:, columns] = (values * inv * gain_ref[:, columns]).astype(jnp.bfloat16)
+
+        by_columns(width, norm)
+        for part in range(2):
+            grams[me, pl.ds(part * block, block), :] = lax.dot_general(
+                normed_ref[pl.ds(part * block, block), :],
+                normed_ref[...],
+                (((1,), (1,)), ((), ())),
+                preferred_element_type=jnp.float32,
+            )
+            for step in steps:
+                gram_copy(me, step, part).start()
+
+    def clip():
+        for step in steps:
+            cot_copy((me + step) % cores, step).wait_recv()
+        gram_values = lax.dot_general(
+            full_ref[...],
+            full_ref[...],
             (((1,), (1,)), ((), ())),
             preferred_element_type=jnp.float32,
         )
+        same_doc = doc_col_ref[...] == doc_row_ref[...]
         for step in steps:
-            gram_copy(me, step, part).start()
-    for step in steps:
-        cot_copy((me + step) % cores, step).wait_recv()
-    gram_values = lax.dot_general(
-        full_ref[...],
-        full_ref[...],
-        (((1,), (1,)), ((), ())),
-        preferred_element_type=jnp.float32,
+            for part in range(2):
+                gram_copy((me + step) % cores, step, part).wait_recv()
+        gram_features = grams[0]
+        for core in range(1, cores):
+            gram_features = gram_features + grams[core]
+        product = jnp.where(same_doc, gram_features * gram_values, 0.0)
+        row_sums = jnp.sum(product, axis=0, keepdims=True)
+        squared = jnp.sum(jnp.where(same_doc, row_sums, 0.0), axis=1, keepdims=True)
+        scales = CLIP_NORM / (jnp.sqrt(squared) + 0.01)
+        clipped_ref[...] = (full_ref[...].astype(jnp.float32) * scales).astype(jnp.bfloat16)
+        for step in steps:
+            cot_copy(me, step).wait_send()
+            square_copy(me, step).wait_send()
+            for part in range(2):
+                gram_copy(me, step, part).wait_send()
+
+    run_gather(
+        links,
+        planes,
+        tile_ref,
+        weight_ref,
+        own_sem,
+        gather_send,
+        gather_recv,
+        [norm_and_grams, clip],
     )
-    same_doc = doc_col_ref[...] == doc_row_ref[...]
-    for step in steps:
-        for part in range(2):
-            gram_copy((me + step) % cores, step, part).wait_recv()
-    gram_features = grams[0]
-    for core in range(1, cores):
-        gram_features = gram_features + grams[core]
-    product = jnp.where(same_doc, gram_features * gram_values, 0.0)
-    row_sums = jnp.sum(product, axis=0, keepdims=True)
-    squared = jnp.sum(jnp.where(same_doc, row_sums, 0.0), axis=1, keepdims=True)
-    scales = CLIP_NORM / (jnp.sqrt(squared) + 0.01)
-    clipped_ref[...] = (full_ref[...].astype(jnp.float32) * scales).astype(jnp.bfloat16)
-    for step in steps:
-        cot_copy(me, step).wait_send()
-        for part in range(2):
-            gram_copy(me, step, part).wait_send()
-
-
-def clip_by_document(normed, cot, doc_ids):
-    tokens, width = cot.shape
+
+
+def gather_and_clip(weight, layer_input, gain_row, cot, doc_ids, count):
+    tokens, cot_width = cot.shape
+    rows, width = weight.shape
     cores = lax.axis_size("mp")
     vmem = pl.BlockSpec(memory_space=pltpu.VMEM)
-    full = jax.ShapeDtypeStruct((tokens, width * cores), cot.dtype)
+    anywhere = pl.BlockSpec(memory_space=pl.ANY)
+    full = jax.ShapeDtypeStruct((tokens, cot_width * cores), cot.dtype)
     return pl.pallas_call(
-        clip_kernel,
-        out_shape=(full, full),
-        in_specs=[vmem] * 4,
-        out_specs=(vmem, vmem),
+        functools.partial(clip_kernel, count // PLANE),
+        out_shape=(
+            jax.ShapeDtypeStruct((count, rows, width), weight.dtype),
+            full,
+            full,
+            jax.ShapeDtypeStruct((tokens, width), jnp.bfloat16),
+            jax.ShapeDtypeStruct((tokens, 1), jnp.float32),
+        ),
+        in_specs=[anywhere, anywhere, vmem, vmem, vmem, vmem],
+        out_specs=(anywhere, vmem, vmem, vmem, vmem),
         scratch_shapes=[
+            pltpu.VMEM((tokens, width), jnp.bfloat16),
+            pltpu.VMEM((cores, tokens, 128), jnp.float32),
             pltpu.VMEM((cores, tokens, tokens), jnp.float32),
-            pltpu.SemaphoreType.DMA((cores - 1, 3)),
-            pltpu.SemaphoreType.DMA((cores, 3)),
+            *gather_scratch(count),
+            pltpu.SemaphoreType.DMA,
+            pltpu.SemaphoreType.DMA((cores - 1, 4)),
+            pltpu.SemaphoreType.DMA((cores, 4)),
         ],
         compiler_params=pltpu.CompilerParams(
             collective_id=3, has_side_effects=True, vmem_limit_bytes=40 * 1024 * 1024
         ),
         cost_estimate=pl.CostEstimate(
-            flops=2 * tokens * tokens * (normed.shape[1] + width * cores),
-            bytes_accessed=2 * tokens * (normed.shape[1] + 4 * width * cores),
+            flops=2 * tokens * tokens * (width + cot_width * cores),
+            bytes_accessed=4 * tokens * width + 4 * count * rows * width,
             transcendentals=0,
         ),
-    )(normed, cot, doc_ids[:, None], doc_ids[None, :])
+    )(weight, layer_input, gain_row, cot, doc_ids[:, None], doc_ids[None, :])
 
 
 def gather_kernel(
@@ -234,9 +469,9 @@
     weighted_ref,
     inner_ref,
     own_sem,
-    weight_sem,
     send_sems,
     recv_sems,
+    weight_sem,
     inner_send,
     inner_recv,
 ):
@@ -246,10 +481,6 @@
     tile = width // 8
     fetch = pltpu.make_async_copy(weight_hbm, weight_ref, weight_sem)
     fetch.start()
-    half = tile_ref.shape[1] // 2
-    mine = links.index(links.line, links.row, links.col)
-    own = pltpu.make_async_copy(tile_ref, out_ref.at[mine], own_sem)
-    own.start()
     links.greet(True)
 
     def inner_copy(slot, step):
@@ -306,101 +537,16 @@
 
         lax.fori_loop(0, 8, at, 0)
 
-    chores = [project_first, project_rest, inner_done]
-
-    def chore():
-        if chores:
-            chores.pop(0)()
-
-    ways = (links.col_peer(), links.row_peer(), links.above(), links.below())
-    pending = []
-
-    def piece(shard, part):
-        return out_ref.at[shard, :, pl.ds(part * half, half)]
-
-    def transfer(shard, part, way, from_tile=False):
-        source = tile_ref.at[:, pl.ds(part * half, half)] if from_tile else piece(shard, part)
-        return remote(
-            source,
-            piece(shard, part),
-            send_sems.at[shard, part, way],
-            recv_sems.at[shard, part],
-            ways[way],
-        )
-
-    def start(shard, part, way, guard, from_tile=False):
-        copy = transfer(shard, part, way, from_tile)
-        pending.append((guard, copy))
-        if guard is None:
-            copy.start()
-        else:
-            pl.when(guard)(copy.start)
-
-    def arrive(shard, part, guard):
-        copy = transfer(shard, part, 0)
-        if guard is None:
-            copy.wait_recv()
-        else:
-            pl.when(guard)(copy.wait_recv)
-
-    def both(first, second):
-        return second if first is None else jnp.logical_and(first, second)
-
-    def spread(line, guard, from_tile):
-        shard = links.index(line, links.row, links.col)
-        start(shard, 0, 0, guard, from_tile)
-        start(shard, 1, 1, guard, from_tile)
-        start(shard, 0, 1, guard, from_tile)
-        start(shard, 1, 0, guard, from_tile)
-
-    def relay(line, guard):
-        shard = links.index(line, links.row, 1 - links.col)
-        arrive(shard, 0, guard)
-        start(shard, 0, 1, guard)
-        shard = links.index(line, 1 - links.row, links.col)
-        arrive(shard, 1, guard)
-        start(shard, 1, 0, guard)
-
-    for part in (0, 1):
-        start(mine, part, 2, links.has_above(), True)
-        start(mine, part, 3, links.has_below(), True)
-    spread(links.line, None, True)
-    chore()
-    lines = [[(links.line, None)]]
-    for step in range(1, planes):
-        from_below = links.line - step
-        from_above = links.line + step
-        got_below = from_below >= 0
-        got_above = from_above < planes
-        for part in (0, 1):
-            shard = links.index(from_below, links.row, links.col)
-            arrive(shard, part, got_below)
-            start(shard, part, 2, both(got_below, links.has_above()))
-            shard = links.index(from_above, links.row, links.col)
-            arrive(shard, part, got_above)
-            start(shard, part, 3, both(got_above, links.has_below()))
-        spread(from_below, got_below, False)
-        spread(from_above, got_above, False)
-        for line, guard in lines[-1]:
-            relay(line, guard)
-        chore()
-        lines.append([(from_below, got_below), (from_above, got_above)])
-    for line, guard in lines[-1]:
-        relay(line, guard)
-    while chores:
-        chore()
-    for group in lines:
-        for line, guard in group:
-            for part in (0, 1):
-                arrive(links.index(line, 1 - links.row, 1 - links.col), part, guard)
-            arrive(links.index(line, 1 - links.row, links.col), 0, guard)
-            arrive(links.index(line, links.row, 1 - links.col), 1, guard)
-    for guard, copy in pending:
-        if guard is None:
-            copy.wait_send()
-        else:
-            pl.when(guard)(copy.wait_send)
-    own.wait()
+    run_gather(
+        links,
+        planes,
+        tile_ref,
+        out_ref,
+        own_sem,
+        send_sems,
+        recv_sems,
+        [project_first, project_rest, inner_done],
+    )
     for step in range(1, cores):
         inner_copy(core, step).wait_send()
 
@@ -423,10 +569,8 @@
             pltpu.VMEM(full_weight.shape, full_weight.dtype),
             pltpu.VMEM((tokens, width), jnp.float32),
             pltpu.VMEM((cores, tokens, 128), jnp.float32),
+            *gather_scratch(count),
             pltpu.SemaphoreType.DMA,
-            pltpu.SemaphoreType.DMA,
-            pltpu.SemaphoreType.DMA((count, 2, 4)),
-            pltpu.SemaphoreType.DMA((count, 2)),
             pltpu.SemaphoreType.DMA((cores - 1,)),
             pltpu.SemaphoreType.DMA((cores,)),
         ],
@@ -707,19 +851,16 @@
     moment_two,
 ):
     part_width = layer_input.shape[1]
-    full_width = part_width * lax.axis_size("mp")
     group_rows = value_weight.shape[0]
     slot_count = master.shape[0] // group_rows
     cycle_size = lax.axis_size("dp")
     my_group = lax.axis_index("dp")
-    inputs = layer_input.astype(jnp.float32)
-    gain_row = norm_gain.astype(jnp.float32)
-    squares = lax.psum(jnp.sum(inputs * inputs, axis=1), "mp")
-    inv_rms = lax.rsqrt(squares / full_width + EPS_NORM)[:, None]
-    normed = (inputs * inv_rms * gain_row).astype(jnp.bfloat16)
+    gain_row = norm_gain.astype(jnp.float32)[None, :]
     seed_value = noise_seeds[my_group]
-    full_weight = lax.all_gather(value_weight, "dp", axis=0, tiled=True)
-    full_cot, clipped = clip_by_document(normed, value_cotangent, doc_ids)
+    full_weight, full_cot, clipped, normed, inv_rms = gather_and_clip(
+        value_weight, layer_input, gain_row, value_cotangent, doc_ids, cycle_size
+    )
+    full_weight = full_weight.reshape(cycle_size * group_rows, part_width)
     group_ids = jnp.arange(cycle_size, dtype=jnp.int32)
     earlier = group_ids[:, None] > group_ids[None, :]
     same_owner = owners[:, None] == owners[None, :]
@@ -731,7 +872,7 @@
     filled_rows = jnp.repeat(filled, group_rows)
     noisy_tile = scatter_sum(clipped, normed, seed_value[None], cycle_size)
     arrived, input_grad = gather_tiles(
-        noisy_tile, cycle_size, full_weight, full_cot, layer_input, gain_row[None, :], inv_rms
+        noisy_tile, cycle_size, full_weight, full_cot, layer_input, gain_row, inv_rms
     )
     gathered = jnp.take(arrived, sources, axis=0).reshape(slot_count * group_rows, part_width)
     gathered = gathered.astype(jnp.float32)

time: 278 us -> 255 us (0.917)
  between operations: 14.2 us -> 0.72 us
  waiting for transfers between devices: 11.5 us -> 0 us
  other arithmetic: 19.3 us -> 12.3 us
  Pallas kernels: 217 us -> 223 us
  local copies, waits for them, and re-layouts: 9.99 us -> 15.4 us
    pallas_call x1, Pallas kernels: 5.24 us -> 64.2 us  [gather_and_clip(): pl.pallas_call(functools.partial(clip_kernel, count // PLANE), out_shape=...]
    pallas_call x1, Pallas kernels: 127 us -> 89.7 us  [scatter_sum(): pl.pallas_call(functools.partial(scatter_kernel, planes), out_shape=jax.S...]
    pallas_call x1, Pallas kernels: 84.4 us -> 69.4 us  [gather_tiles(): pl.pallas_call(functools.partial(gather_kernel, count // PLANE), out_shap...]
    all_gather x1 -> x0, waiting for transfers between devices: 10.9 us -> none  [body(): full_weight = lax.all_gather(value_weight, 'dp', axis=0, tiled=True)]
    unnamed x13 -> x15, local copies, waits for them, and re-layouts: 4.05 us -> 8.98 us
    convert_element_type x2 -> x0, other arithmetic: 4.58 us -> none  [the longest x1 3.88 us: body(): normed = (inputs * inv_rms * gain_row).astype(jnp.bfloat16)]
    reduce_sum x1 -> x0, other arithmetic: 3.09 us -> none  [body(): squares = lax.psum(jnp.sum(inputs * inputs, axis=1), 'mp')]
  transfers between devices with their start and end apart: 1 -> 0, of which waited for: 1 -> 0; matrix products, arithmetic and copies ran while one was open for 4% -> 0% of each run, Pallas kernels for 48% -> 0%
where the time goes in v3:
time: 255 us; the launch traced here: 252 us
  Pallas kernels  223 us (87%)
  local copies, waits for them, and re-layouts  15.4 us (6%)
  other arithmetic  12.3 us (5%)
    pallas_call x1, Pallas kernels, scatter_sum(): pl.pallas_call(functools.partial(scatter_kernel, planes), out_shape=jax.S...  89.7 us
    pallas_call x1, Pallas kernels, gather_tiles(): pl.pallas_call(functools.partial(gather_kernel, count // PLANE), out_shap...  69.4 us
    pallas_call x1, Pallas kernels, gather_and_clip(): pl.pallas_call(functools.partial(clip_kernel, count // PLANE), out_shape=...  64.2 us
    select_n x1, other arithmetic, body(): new_moment_two = jnp.where(keep_mask, second_new, moment_two)  11.2 us
    unnamed x15, local copies, waits for them, and re-layouts  8.98 us

profile of v3, /device:TPU:28, one launch (start us, length us, event | category | flops | bytes accessed | tf_op | source)
XLA Modules:
  0.0 251.7 jit_solution(14271567124339612658)
XLA Ops:
  0.6 1.2 dynamic_slice.3.seed_ref
  1.9 0.7 broadcast_in_dim.77
  2.6 0.8 copy.15.doc_col_ref
  3.4 0.0 copy-start.2
  3.4 0.7 copy-done.2
  4.1 2.2 copy-done.3
  6.3 1.0 copy-done.4
  7.3 1.0 copy-done.5
  8.4 64.2 %shard_map.129 = (bf16[16,64,4096]{2,1,0:T(8,128)(2,1)}, bf16[512,1024]{1,0:T(8,128)(2,1)S(1)}, bf16[512,1024]{1,0:T(8,128)(2,1)S(1)}, bf16[512,4096]{1,0:T(8,128)(2,1)S(1)}, f32[512,1]{1,0:T(8,128)S(1)}) custom-call(bf16[64,4096]{1,0:T(8,128)(2,1)S(1)} %copy-done.4, bf16[512,4096]{1,0:T(8,128)(2,1)S(1)} %copy-done.3, f32[1,4096]{1,0:T(1,128)S(1)} %bitcast.16, ...), custom_call_target="tpu_custom_call" | custom-call | flops 2684354560 | bytes 25165824 | tf_op jit(solution)/shard_map/pallas_call | solution.py:427
  72.5 89.7 %shard_map.130.tile_ref = bf16[64,4096]{1,0:T(8,128)(2,1)S(1)} custom-call(bf16[512,1024]{1,0:T(8,128)(2,1)S(1)} %get-tuple-element.11.clipped_ref, bf16[512,4096]{1,0:T(8,128)(2,1)S(1)} %get-tuple-element.12.normed_ref, s32[1]{0:T(128)} %dynamic_slice.3.seed_ref), custom_call_target="tpu_custom_call" | custom-call | flops 4294967296 | bytes 33554432 | tf_op jit(solution)/shard_map/pallas_call | solution.py:812
  162.2 0.0 copy-start.6
  162.2 69.4 %shard_map.131 = (bf16[16,64,4096]{2,1,0:T(8,128)(2,1)}, bf16[512,4096]{1,0:T(8,128)(2,1)S(1)}) custom-call(bf16[64,4096]{1,0:T(8,128)(2,1)S(1)} %shard_map.130.tile_ref, bf16[1024,4096]{1,0:T(8,128)(2,1)} %bitcast.20, bf16[512,1024]{1,0:T(8,128)(2,1)S(1)} %get-tuple-element.14.cot_ref, bf16[512,4096]{1,0:T(8,128)(2,1)} %input_ref.1, ...), custom_call_target="tpu_custom_call" | custom-call | flops 4294967296 | bytes 25165824 | tf_op jit(solution)/shard_map/pallas_call | solution.py:560
  231.6 0.0 copy-start
  231.6 2.0 copy-done
  233.6 0.2 convert_reduce_fusion
  233.8 0.1 select_reduce_fusion
  234.0 4.1 %gather_fusion = bf16[4,64,4096]{2,1,0:T(8,128)(2,1)S(1)} fusion(bf16[16,64,4096]{2,1,0:T(8,128)(2,1)} %get-tuple-element.17, s32[1024]{0:T(1024)S(1)} %pad_clamp_fusion), kind=kCustom, calls=%fused_computation | custom fusion | bytes 4194320 | tf_op jit(solution)/shard_map/jit(_take)/gather | solution.py:877
  238.1 0.1 broadcast_in_dim.73
  238.1 0.1 broadcast_in_dim.74
  238.2 0.1 fusion.6
  238.3 0.1 broadcast_in_dim.68
  238.4 0.1 broadcast_in_dim.69
  238.5 11.2 %fusion.2 = (f32[256,4096]{1,0:T(8,128)}, f32[256,4096]{1,0:T(8,128)}, f32[256,4096]{1,0:T(8,128)}) fusion(f32[256,4096]{1,0:T(8,128)} %param.19, pred[256]{0:T(512)(128)(4,1)S(1)} %broadcast_in_dim.69, bf16[4,64,4096]{2,1,0:T(8,128)(2,1)S(1)} %gather_fusion, pred[256]{0:T(512)(128)(4,1)S(1)} %broadcast_in_dim.74, f32[256,4096]{1,0:T(8,128)} %param.17, ...), kind=kLoop, calls=%fused_computation.6 | loop fusion | flops 18874368 | bytes 27263488 | tf_op jit(solution)/shard_map/jit(_where)/select_n | solution.py:890
  249.7 2.0 copy.17
  (10 shorter events, 0.0 us)
Async XLA Ops:
  3.4 0.7 copy-start.2
  4.1 2.2 copy-start.3
  6.3 1.0 copy-start.4
  7.3 1.0 copy-start.5
  162.2 71.4 %copy-start.6 = (s32[16]{0:T(128)S(1)}, s32[16]{0:T(128)}, u32[]{:S(2)}) copy-start(s32[16]{0:T(128)} %param.15) | copy-start | bytes 196
  231.6 2.0 copy-start
  238.5 11.2 %copy-start.1 = (bf16[512,4096]{1,0:T(8,128)(2,1)S(1)}, bf16[512,4096]{1,0:T(8,128)(2,1)}, u32[]{:S(2)}) copy-start(bf16[512,4096]{1,0:T(8,128)(2,1)} %copy-done) | copy-start | bytes 12582916

commit v4 on v3

--- a/solution.py
+++ b/solution.py
@@ -113,10 +113,13 @@
     )
 
 
+def column_parts(width):
+    extra = 2 * ((width // 128) * 3 // 32) * 128
+    return (width - extra) // 2, extra
+
+
 def run_gather(links, planes, tile_ref, out_ref, own_sem, send_sems, recv_sems, chores):
-    width = tile_ref.shape[1]
-    extra = 2 * ((width // 128) * 3 // 32) * 128
-    half = (width - extra) // 2
+    half, extra = column_parts(tile_ref.shape[1])
     spans = (pl.ds(0, half), pl.ds(half, half), pl.ds(2 * half, extra))
     line, row, col = links.line, links.row, links.col
     mine = links.index(line, row, col)
@@ -598,14 +601,25 @@
     line_in,
     second_out,
     line_out,
+    far_in,
+    far_out,
+    cross_in,
+    cross_out,
+    cross_keep,
+    last_in,
+    last_out,
     send_sems,
     first_sems,
     second_sems,
     line_sems,
+    far_send,
+    far_sems,
+    cross_sems,
 ):
     links = Links(planes)
     rows, width = out_ref.shape
-    half = width // 2
+    half, extra = column_parts(width)
+    rest = pl.ds(2 * half, extra)
     block = 16
     links.greet()
     pending = []
@@ -764,19 +778,123 @@
                 pl.when(sends)(copy.start)
                 pending.append((sends, copy))
 
+    def far_sides(line):
+        return ((0, place < line, place > 0), (1, place > line, place < planes - 1))
+
+    def far_copy(line, side, source):
+        return remote(
+            source,
+            far_in.at[side, line],
+            far_send.at[line],
+            far_sems.at[side, line],
+            links.above() if side == 0 else links.below(),
+        )
+
+    def far_start(line):
+        for side, sends, joins in far_sides(line):
+            guard = jnp.logical_and(sends, jnp.logical_not(joins))
+            copy = far_copy(line, side, part_ref.at[line, :, :, :, rest])
+            pl.when(guard)(copy.start)
+            pending.append((guard, copy))
+
+    def far_join(line):
+        for side, sends, joins in far_sides(line):
+            guard = jnp.logical_and(sends, joins)
+            copy = far_copy(line, side, far_out.at[line])
+            pending.append((guard, copy))
+
+            @pl.when(guard)
+            def _():
+                copy.wait_recv()
+
+                def step(at):
+                    for lane in range(PLANE):
+                        up, left = lane // 2, lane % 2
+                        far_out[line, up, left, at, :] = (
+                            part_ref[line, up, left, at, rest].astype(jnp.float32)
+                            + far_in[side, line, up, left, at, :].astype(jnp.float32)
+                        ).astype(jnp.bfloat16)
+
+                by_blocks(step)
+                copy.start()
+
+    def cross_copy():
+        return remote(
+            cross_out, cross_in, cross_sems.at[0], cross_sems.at[1], links.col_peer()
+        )
+
+    def last_copy():
+        return remote(last_out, last_in, cross_sems.at[2], cross_sems.at[3], links.row_peer())
+
+    def far_sum():
+        for side, joins in ((0, place > 0), (1, place < planes - 1)):
+            pl.when(joins)(far_copy(place, side, far_out.at[place]).wait_recv)
+
+        def step(at):
+            for up in range(2):
+                for give, left in ((True, 1 - col), (False, col)):
+                    total = part_ref[place, up, left, at, rest].astype(jnp.float32)
+                    for side, joins in ((0, place > 0), (1, place < planes - 1)):
+                        came = far_in[side, place, up, left, at, :].astype(jnp.float32)
+                        total = total + jnp.where(joins, came, 0.0)
+                    if give:
+                        cross_out[up, at, :] = total.astype(jnp.bfloat16)
+                    else:
+                        cross_keep[up, at, :] = total
+
+        by_blocks(step)
+        cross_copy().start()
+        pending.append((None, cross_copy()))
+
+    def cross_sum():
+        cross_copy().wait_recv()
+
+        def step(at):
+            last_out[at, :] = (
+                cross_keep[1 - row, at, :] + cross_in[1 - row, at, :].astype(jnp.float32)
+            ).astype(jnp.bfloat16)
+            total_ref[at, rest] += cross_keep[row, at, :] + cross_in[row, at, :].astype(
+                jnp.float32
+            )
+
+        by_blocks(step)
+        last_copy().start()
+        pending.append((None, last_copy()))
+
+    def last_sum():
+        last_copy().wait_recv()
+
+        def step(at):
+            total_ref[at, rest] += last_in[at, :].astype(jnp.float32)
+
+        by_blocks(step)
+
     ahead = 2
-    for line in order[:ahead]:
+    for index, line in enumerate(order):
         make_tiles(line)
-        send_first(line)
+        if index < ahead:
+            send_first(line)
+        if extra:
+            far_start(line)
     draw_noise()
+    joined = 0
     for index, line in enumerate(order):
         send_second(line)
         if index + ahead < planes:
-            make_tiles(order[index + ahead])
             send_first(order[index + ahead])
+        if extra:
+            for later in order[joined : joined + 2]:
+                far_join(later)
+            joined += 2
+            if index == planes - 2:
+                far_sum()
+            if index == planes - 1:
+                cross_sum()
         if index > 0:
             send_line(order[index - 1])
     send_line(order[-1])
+    if extra:
+        last_sum()
 
     for side, joins in ((0, place > 0), (1, place < planes - 1)):
         for part in (0, 1):
@@ -808,7 +926,8 @@
     rows = clipped.shape[1] // count
     width = normed.shape[1]
     vmem = pl.BlockSpec(memory_space=pltpu.VMEM)
-    half = width // 2
+    half, extra = column_parts(width)
+    spare = max(extra, 128)
     return pl.pallas_call(
         functools.partial(scatter_kernel, planes),
         out_shape=jax.ShapeDtypeStruct((rows, width), jnp.bfloat16),
@@ -822,13 +941,23 @@
             pltpu.VMEM((2, planes, 2, rows, half), jnp.bfloat16),
             pltpu.VMEM((planes, 2, rows, half), jnp.bfloat16),
             pltpu.VMEM((planes, 2, rows, half), jnp.bfloat16),
+            pltpu.VMEM((2, planes, 2, 2, rows, spare), jnp.bfloat16),
+            pltpu.VMEM((planes, 2, 2, rows, spare), jnp.bfloat16),
+            pltpu.VMEM((2, rows, spare), jnp.bfloat16),
+            pltpu.VMEM((2, rows, spare), jnp.bfloat16),
+            pltpu.VMEM((2, rows, spare), jnp.float32),
+            pltpu.VMEM((rows, spare), jnp.bfloat16),
+            pltpu.VMEM((rows, spare), jnp.bfloat16),
             pltpu.SemaphoreType.DMA((planes, 2, 3)),
             pltpu.SemaphoreType.DMA((planes, 2)),
             pltpu.SemaphoreType.DMA((planes, 2)),
             pltpu.SemaphoreType.DMA((2, planes, 2)),
+            pltpu.SemaphoreType.DMA((planes,)),
+            pltpu.SemaphoreType.DMA((2, planes)),
+            pltpu.SemaphoreType.DMA((4,)),
         ],
         compiler_params=pltpu.CompilerParams(
-            collective_id=2, has_side_effects=True, vmem_limit_bytes=40 * 1024 * 1024
+            collective_id=2, has_side_effects=True, vmem_limit_bytes=48 * 1024 * 1024
         ),
         cost_estimate=pl.CostEstimate(
             flops=2 * count * rows * width * clipped.shape[0],
@@ -836,6 +965,78 @@
             transcendentals=0,
         ),
     )(clipped, normed, seed)
+
+
+def adam_kernel(
+    sources_ref,
+    filled_ref,
+    noisy_ref,
+    master_ref,
+    first_ref,
+    second_ref,
+    new_master_ref,
+    new_first_ref,
+    new_second_ref,
+):
+    rows, width = master_ref.shape
+    filled = filled_ref[pl.program_id(0)] != 0
+    tile = min(width, 512)
+    across = width // tile
+
+    @pl.when(filled)
+    def _():
+        def at(index, carry):
+            span = (
+                pl.ds(pl.multiple_of((index // across) * 16, 16), 16),
+                pl.ds(pl.multiple_of((index % across) * tile, tile), tile),
+            )
+            noisy = noisy_ref[(0,) + span].astype(jnp.float32)
+            first_new = BETA_ONE * first_ref[span] + (1.0 - BETA_ONE) * noisy
+            second_new = BETA_TWO * second_ref[span] + (1.0 - BETA_TWO) * noisy * noisy
+            update = (first_new * (1.0 / (1.0 - BETA_ONE**ADAM_STEP))) / (
+                jnp.sqrt(second_new * (1.0 / (1.0 - BETA_TWO**ADAM_STEP))) + ADAM_EPS
+            )
+            new_master_ref[span] = master_ref[span] - LEARN_RATE * update
+            new_first_ref[span] = first_new
+            new_second_ref[span] = second_new
+            return carry
+
+        lax.fori_loop(0, (rows // 16) * across, at, 0)
+
+    @pl.when(jnp.logical_not(filled))
+    def _():
+        new_master_ref[...] = master_ref[...]
+        new_first_ref[...] = first_ref[...]
+        new_second_ref[...] = second_ref[...]
+
+
+def adam_update(sources, filled, noisy, master, moment_one, moment_two):
+    slots = sources.shape[0]
+    rows, width = noisy.shape[1:]
+    tile = min(width, 2048)
+    state = pl.BlockSpec((rows, tile), lambda slot, part, source, full: (slot, part))
+    shape = jax.ShapeDtypeStruct(master.shape, master.dtype)
+    return pl.pallas_call(
+        adam_kernel,
+        out_shape=(shape, shape, shape),
+        grid_spec=pltpu.PrefetchScalarGridSpec(
+            num_scalar_prefetch=2,
+            grid=(slots, width // tile),
+            in_specs=[
+                pl.BlockSpec(
+                    (1, rows, tile), lambda slot, part, source, full: (source[slot], 0, part)
+                ),
+                state,
+                state,
+                state,
+            ],
+            out_specs=[state, state, state],
+        ),
+        compiler_params=pltpu.CompilerParams(vmem_limit_bytes=24 * 1024 * 1024),
+        cost_estimate=pl.CostEstimate(
+            flops=15 * master.size, bytes_accessed=26 * master.size, transcendentals=0
+        ),
+    )(sources, filled, noisy, master, moment_one, moment_two)
 
 
 def body(
@@ -869,25 +1070,13 @@
     holds_slot = (owners[None, :] == my_group) & (slot_rank[None, :] == slot_ids[:, None])
     sources = jnp.sum(jnp.where(holds_slot, group_ids[None, :], 0), axis=1)
     filled = jnp.any(holds_slot, axis=1)
-    filled_rows = jnp.repeat(filled, group_rows)
     noisy_tile = scatter_sum(clipped, normed, seed_value[None], cycle_size)
     arrived, input_grad = gather_tiles(
         noisy_tile, cycle_size, full_weight, full_cot, layer_input, gain_row, inv_rms
     )
-    gathered = jnp.take(arrived, sources, axis=0).reshape(slot_count * group_rows, part_width)
-    gathered = gathered.astype(jnp.float32)
-    first_new = BETA_ONE * moment_one + (1.0 - BETA_ONE) * gathered
-    second_new = BETA_TWO * moment_two + (1.0 - BETA_TWO) * gathered * gathered
-    update = (
-        first_new
-        / (1.0 - BETA_ONE**ADAM_STEP)
-        / (jnp.sqrt(second_new / (1.0 - BETA_TWO**ADAM_STEP)) + ADAM_EPS)
+    new_master, new_moment_one, new_moment_two = adam_update(
+        sources, filled.astype(jnp.int32), arrived, master, moment_one, moment_two
     )
-    master_new = master - LEARN_RATE * update
-    keep_mask = filled_rows[:, None]
-    new_master = jnp.where(keep_mask, master_new, master)
-    new_moment_one = jnp.where(keep_mask, first_new, moment_one)
-    new_moment_two = jnp.where(keep_mask, second_new, moment_two)
     return (input_grad, new_master, new_moment_one, new_moment_two)
 
 

time: 255 us -> 241 us (0.945)
  other arithmetic: 12.3 us -> 2.52 us
  Pallas kernels: 223 us -> 218 us
    pallas_call x1, Pallas kernels: 89.7 us -> 78.4 us  [scatter_sum(): pl.pallas_call(functools.partial(scatter_kernel, planes), out_shape=jax.S...]
    select_n x2 -> x0, other arithmetic: 11.2 us -> none  [the longest x1 11.2 us: body(): new_moment_two = jnp.where(keep_mask, second_new, moment_two)]
    pallas_call x0 -> x1, Pallas kernels: none -> 6.69 us  [adam_update(): pl.pallas_call(adam_kernel, out_shape=(shape, shape, shape), grid_spec=pl...]
    gather x1 -> x0, local copies, waits for them, and re-layouts: 4.06 us -> none  [body(): jnp.take(arrived, sources, axis=0)]
    unnamed x15 -> x17, local copies, waits for them, and re-layouts: 8.98 us -> 12.5 us
where the time goes in v4:
time: 241 us; the launch traced here: 236 us
  Pallas kernels  218 us (90%)
  local copies, waits for them, and re-layouts  14.6 us (6%)
  other arithmetic  2.52 us (1%)
    pallas_call x1, Pallas kernels, scatter_sum(): pl.pallas_call(functools.partial(scatter_kernel, planes), out_shape=jax.S...  78.4 us
    pallas_call x1, Pallas kernels, gather_tiles(): pl.pallas_call(functools.partial(gather_kernel, count // PLANE), out_shap...  68.7 us
    pallas_call x1, Pallas kernels, gather_and_clip(): pl.pallas_call(functools.partial(clip_kernel, count // PLANE), out_shape=...  64.2 us
    unnamed x17, local copies, waits for them, and re-layouts  12.5 us
    pallas_call x1, Pallas kernels, adam_update(): pl.pallas_call(adam_kernel, out_shape=(shape, shape, shape), grid_spec=pl...  6.69 us

profile of v4, /device:TPU:28, one launch (start us, length us, event | category | flops | bytes accessed | tf_op | source)
XLA Modules:
  0.0 235.8 jit_solution(2728863349579582337)
XLA Ops:
  0.6 0.7 broadcast_compare_fusion
  1.3 1.2 dynamic_slice.3.seed_ref
  2.5 0.9 convert_reduce_fusion
  3.4 0.1 fusion.2
  3.6 0.1 select_reduce_fusion.sources_ref
  3.7 0.7 broadcast_in_dim.37
  4.4 0.8 copy.15.doc_col_ref
  5.2 0.0 copy-start.4
  5.2 0.7 copy-done.4
  5.9 2.2 copy-done.5
  8.1 1.0 copy-done.6
  9.1 1.0 copy-done.7
  10.2 64.2 %shard_map.129 = (bf16[16,64,4096]{2,1,0:T(8,128)(2,1)}, bf16[512,1024]{1,0:T(8,128)(2,1)S(1)}, bf16[512,1024]{1,0:T(8,128)(2,1)S(1)}, bf16[512,4096]{1,0:T(8,128)(2,1)S(1)}, f32[512,1]{1,0:T(8,128)S(1)}) custom-call(bf16[64,4096]{1,0:T(8,128)(2,1)S(1)} %copy-done.6, bf16[512,4096]{1,0:T(8,128)(2,1)S(1)} %copy-done.5, f32[1,4096]{1,0:T(1,128)S(1)} %bitcast.4, ...), custom_call_target="tpu_custom_call" | custom-call | flops 2684354560 | bytes 25165824 | tf_op jit(solution)/shard_map/pallas_call | solution.py:430
  74.4 78.4 %shard_map.130.tile_ref = bf16[64,4096]{1,0:T(8,128)(2,1)S(1)} custom-call(bf16[512,1024]{1,0:T(8,128)(2,1)S(1)} %get-tuple-element.14.clipped_ref, bf16[512,4096]{1,0:T(8,128)(2,1)S(1)} %get-tuple-element.15.normed_ref, s32[1]{0:T(128)} %dynamic_slice.3.seed_ref), custom_call_target="tpu_custom_call" | custom-call | flops 4294967296 | bytes 33554432 | tf_op jit(solution)/shard_map/pallas_call | solution.py:931
  152.7 0.0 copy-start.1
  152.7 0.0 copy-start.2
  152.8 68.7 %shard_map.131 = (bf16[16,64,4096]{2,1,0:T(8,128)(2,1)}, bf16[512,4096]{1,0:T(8,128)(2,1)S(1)}) custom-call(bf16[64,4096]{1,0:T(8,128)(2,1)S(1)} %shard_map.130.tile_ref, bf16[1024,4096]{1,0:T(8,128)(2,1)} %bitcast.8, bf16[512,1024]{1,0:T(8,128)(2,1)S(1)} %get-tuple-element.17.cot_ref, bf16[512,4096]{1,0:T(8,128)(2,1)} %input_ref.1, f32[1,4096]{1,0:T(1,128)S(1)} %bitcast.5, ...), custom_call_target="tpu_custom_call" | custom-call | flops 4294967296 | bytes 25165824 | tf_op jit(solution)/shard_map/pallas_call | solution.py:563
  221.5 0.0 copy-done.1
  221.5 0.0 copy-done.2
  221.5 0.0 copy-start
  221.5 3.4 %copy-done = bf16[16,64,4096]{2,1,0:T(8,128)(2,1)S(1)} copy-done((bf16[16,64,4096]{2,1,0:T(8,128)(2,1)S(1)}, bf16[16,64,4096]{2,1,0:T(8,128)(2,1)}, u32[]{:S(2)}) %copy-start) | copy-done | bytes 8388632
  224.9 2.2 copy-done.3
  227.1 6.7 %shard_map.132 = (f32[256,4096]{1,0:T(8,128)}, f32[256,4096]{1,0:T(8,128)}, f32[256,4096]{1,0:T(8,128)}) custom-call(s32[4]{0:T(128)S(1)} %select_reduce_fusion.sources_ref, s32[4]{0:T(128)S(1)} %convert_element_type.8.filled_ref, bf16[16,64,4096]{2,1,0:T(8,128)(2,1)S(1)} %copy-done, f32[256,4096]{1,0:T(8,128)S(1)} %copy-done.1, f32[256,4096]{1,0:T(8,128)S(1)} %copy-done.2, ...), custom_call_target="tpu_custom_call" | custom-call | flops 15728640 | bytes 27262976 | tf_op jit(solution)/shard_map/pallas_call | solution.py:1019
  233.8 2.0 copy.17
  (5 shorter events, 0.0 us)
Async XLA Ops:
  5.2 0.7 copy-start.4
  5.9 2.2 copy-start.5
  8.1 1.0 copy-start.6
  9.1 1.0 copy-start.7
  152.7 68.8 %copy-start.1 = (f32[256,4096]{1,0:T(8,128)S(1)}, f32[256,4096]{1,0:T(8,128)}, u32[]{:S(2)}) copy-start(f32[256,4096]{1,0:T(8,128)} %master_ref.1) | copy-start | bytes 12582916
  152.7 68.8 %copy-start.2 = (f32[256,4096]{1,0:T(8,128)S(1)}, f32[256,4096]{1,0:T(8,128)}, u32[]{:S(2)}) copy-start(f32[256,4096]{1,0:T(8,128)} %first_ref.1) | copy-start | bytes 12582916
  221.5 3.4 %copy-start = (bf16[16,64,4096]{2,1,0:T(8,128)(2,1)S(1)}, bf16[16,64,4096]{2,1,0:T(8,128)(2,1)}, u32[]{:S(2)}) copy-start(bf16[16,64,4096]{2,1,0:T(8,128)(2,1)} %get-tuple-element.20.noisy_ref) | copy-start | bytes 25165828
  224.9 2.2 copy-start.3
